TPU v7x, 128 devices: a whole 4x4x4 slice. The times are simulated.
128 devices in a mesh: dp: 32 (over x_lo, z, y), tensor: 4 (over x_hi, core).
Axes of the slice: x: 4 (x_hi: 2, x_lo: 2; x = x_hi * 2 + x_lo), y: 4, z: 4, core: 2. Of those that a mesh axis runs over, the one named last changes fastest.
Arguments:
- tokens: bfloat16 [16384, 1024], P(('dp', 'tensor')), may hold values from -6 to 6
- seq_lens: int32 [32, 4], P('dp'), may hold values from 1 to 509, as said below
- norm_attn: float32 [1024], replicated, may hold values from 0.25 to 1.75
- w_query: bfloat16 [1024, 1024], P('dp', 'tensor'), may hold values from -0.1875 to 0.1875
- w_key: bfloat16 [1024, 512], P('dp', 'tensor'), may hold values from -0.1875 to 0.1875
- w_value: bfloat16 [1024, 512], P('dp', 'tensor'), may hold values from -0.1875 to 0.1875
- w_out: bfloat16 [1024, 1024], P('tensor', 'dp'), may hold values from -3 to 3
- query_gain: float32 [64], replicated, may hold values from 0.25 to 1.75
- key_gain: float32 [64], replicated, may hold values from 0.25 to 1.75
- norm_ffn: float32 [1024], replicated, may hold values from 0.25 to 1.75
- w_gate: bfloat16 [1024, 4608], P('dp', 'tensor'), may hold values from -0.1875 to 0.1875
- w_up: bfloat16 [1024, 4608], P('dp', 'tensor'), may hold values from -0.1875 to 0.1875
- w_down: bfloat16 [4608, 1024], P('tensor', 'dp'), may hold values from -0.09375 to 0.09375
- cotangent: bfloat16 [16384, 1024], P(('dp', 'tensor')), may hold values from -6 to 6
Outputs:
- output: bfloat16 [16384, 1024], P(('dp', 'tensor'))
- grad_tokens: float32 [16384, 1024], P(('dp', 'tensor'))
- grad_norm_attn: float32 [1024], replicated
- grad_w_query: float32 [1024, 1024], P('dp', 'tensor')
- grad_w_key: float32 [1024, 512], P('dp', 'tensor')
- grad_w_value: float32 [1024, 512], P('dp', 'tensor')
- grad_w_out: float32 [1024, 1024], P('tensor', 'dp')
- grad_query_gain: float32 [64], replicated
- grad_key_gain: float32 [64], replicated
- grad_norm_ffn: float32 [1024], replicated
- grad_w_gate: float32 [1024, 4608], P('dp', 'tensor')
- grad_w_up: float32 [1024, 4608], P('dp', 'tensor')
- grad_w_down: float32 [4608, 1024], P('tensor', 'dp')
Inputs may be any that keep to these rules, and one draw needn't show every extreme that they name: `seq_lens`: each row lists the lengths of the 4 sequences of one dp rank in packing order; they sum to 512, and one of them is longer than 384.
All inputs are finite; a program needn't handle non-finite values.
Results may differ from a plain program's by a relative error of at most 0.025.
Values may be sent and summed in bfloat16 or wider, within the bound.
A program may use at most 128 MiB of HBM per device.

v0:
```python
import math

import jax
import jax.numpy as jnp
from jax import lax
from jax.sharding import PartitionSpec as P

BLOCK = 512


epsilon = 1e-05
theta = 1000000.0


def mult(left, right):
    return jnp.dot(left, right, preferred_element_type=jnp.float32)


def mult_nt(left, right):
    return lax.dot_general(
        left, right, (((1,), (1,)), ((), ())), preferred_element_type=jnp.float32
    )


def mult_tn(left, right):
    return lax.dot_general(
        left, right, (((0,), (0,)), ((), ())), preferred_element_type=jnp.float32
    )


def normalize(values):
    inverse = lax.rsqrt(jnp.mean(values * values, axis=-1, keepdims=True) + epsilon)
    return (values * inverse, inverse)


def norm_back(grad_norm, normed, inverse):
    return inverse * (grad_norm - normed * jnp.mean(grad_norm * normed, axis=-1, keepdims=True))


def layout(seq_lens, rows):
    ends = jnp.cumsum(seq_lens)
    starts = ends - seq_lens
    index = jnp.arange(rows, dtype=jnp.int32)
    segment = jnp.sum((index[:, None] >= ends[None, :]).astype(jnp.int32), axis=1)
    owner = segment[:, None] == jnp.arange(seq_lens.shape[0], dtype=jnp.int32)[None, :]
    offset = jnp.sum(jnp.where(owner, starts[None, :], 0), axis=1)
    return (segment, index - offset)


def tables(position, width):
    half = width // 2
    freq = jnp.exp(-math.log(theta) * 2.0 * jnp.arange(half, dtype=jnp.float32) / width)
    angle = position.astype(jnp.float32)[:, None] * freq[None, :]
    return (jnp.cos(angle)[:, None, :], jnp.sin(angle)[:, None, :])


def rotate(values, cosine, sine):
    half = values.shape[-1] // 2
    first = values[..., :half]
    second = values[..., half:]
    return jnp.concatenate(
        [first * cosine - second * sine, second * cosine + first * sine], axis=-1
    )


def rotate_back(grads, cosine, sine):
    half = grads.shape[-1] // 2
    first = grads[..., :half]
    second = grads[..., half:]
    return jnp.concatenate(
        [first * cosine + second * sine, second * cosine - first * sine], axis=-1
    )


def visible(segment, start, count):
    rows = segment.shape[0]
    query_index = start + jnp.arange(count, dtype=jnp.int32)
    key_index = jnp.arange(rows, dtype=jnp.int32)
    return (segment[:, None] == segment[None, :]) & (key_index[None, :] <= query_index[:, None])


def block_scores(qblock, start, key_rot, segment):
    scale = qblock.shape[-1] ** (-0.5)
    raw = jnp.einsum("bkgd,skd->kgbs", qblock, key_rot, preferred_element_type=jnp.float32)
    allowed = visible(segment, start, qblock.shape[0])
    return (jnp.where(allowed, raw * scale, -1e30), scale)


def attend_block(qblock, start, key_rot, value_rot, segment):
    scores, scale = block_scores(qblock, start, key_rot, segment)
    top = jnp.max(scores, axis=-1, keepdims=True)
    expo = jnp.exp(scores - top)
    total = jnp.sum(expo, axis=-1, keepdims=True)
    probs = (expo / total).astype(jnp.bfloat16)
    result = jnp.einsum("kgbs,skd->bkgd", probs, value_rot, preferred_element_type=jnp.float32)
    return (result.astype(jnp.bfloat16), (top + jnp.log(total))[..., 0])


def on_device(
    tokens,
    seq_lens,
    norm_attn,
    w_query,
    w_key,
    w_value,
    w_out,
    query_gain,
    key_gain,
    norm_ffn,
    w_gate,
    w_up,
    w_down,
    cotangent,
):
    head = query_gain.shape[0]
    resid = tokens.astype(jnp.float32)
    query_full, key_full, value_full, out_full = (
        lax.all_gather(w_query, "dp", axis=0, tiled=True),
        lax.all_gather(w_key, "dp", axis=0, tiled=True),
        lax.all_gather(w_value, "dp", axis=0, tiled=True),
        lax.all_gather(w_out, "dp", axis=1, tiled=True),
    )
    normed_one, inverse_one = normalize(resid)
    input_one = (normed_one * norm_attn).astype(jnp.bfloat16)
    gathered_one = lax.all_gather(input_one, "tensor", axis=0, tiled=True)
    rows = gathered_one.shape[0]
    segment, position = layout(seq_lens[0], rows)
    cosine, sine = tables(position, head)
    q_heads = query_full.shape[1] // head
    k_heads = key_full.shape[1] // head
    group = q_heads // k_heads
    query_raw = mult(gathered_one, query_full).reshape(rows, q_heads, head)
    key_raw = mult(gathered_one, key_full).reshape(rows, k_heads, head)
    value_rot = mult(gathered_one, value_full).astype(jnp.bfloat16).reshape(rows, k_heads, head)
    query_normed, query_inverse = normalize(query_raw)
    key_normed, key_inverse = normalize(key_raw)
    query_rot = rotate(query_normed * query_gain, cosine, sine).astype(jnp.bfloat16)
    key_rot = rotate(key_normed * key_gain, cosine, sine).astype(jnp.bfloat16)
    count = rows // BLOCK
    starts = jnp.arange(count, dtype=jnp.int32) * BLOCK
    query_blocks = query_rot.reshape(count, BLOCK, k_heads, group, head)

    def forward_block(item):
        return attend_block(item[0], item[1], key_rot, value_rot, segment)

    attended, lse = lax.map(forward_block, (query_blocks, starts))
    attended = attended.reshape(rows, q_heads * head)
    attn_out = lax.psum_scatter(mult(attended, out_full), "tensor", scatter_dimension=0, tiled=True)
    middle = resid + attn_out
    gate_full, up_full, down_full = (
        lax.all_gather(w_gate, "dp", axis=0, tiled=True),
        lax.all_gather(w_up, "dp", axis=0, tiled=True),
        lax.all_gather(w_down, "dp", axis=1, tiled=True),
    )
    normed_two, inverse_two = normalize(middle)
    input_two = (normed_two * norm_ffn).astype(jnp.bfloat16)
    gathered_two = lax.all_gather(input_two, "tensor", axis=0, tiled=True)
    gate = mult(gathered_two, gate_full)
    up = mult(gathered_two, up_full)
    sigma = jax.nn.sigmoid(gate)
    swish = gate * sigma
    hidden = (swish * up).astype(jnp.bfloat16)
    ffn_out = lax.psum_scatter(
        mult(hidden, down_full).astype(jnp.bfloat16), "tensor", scatter_dimension=0, tiled=True
    ).astype(jnp.float32)
    output = (middle + ffn_out).astype(jnp.bfloat16)
    grad_out = cotangent.astype(jnp.float32)
    grad_rows = lax.all_gather(cotangent, "tensor", axis=0, tiled=True)
    grad_down = mult_tn(hidden, grad_rows)
    grad_hidden = mult_nt(grad_rows, down_full)
    grad_gate = (grad_hidden * up * sigma * (1.0 + gate * (1.0 - sigma))).astype(jnp.bfloat16)
    grad_up = (grad_hidden * swish).astype(jnp.bfloat16)
    grad_gate_w = mult_tn(gathered_two, grad_gate)
    grad_up_w = mult_tn(gathered_two, grad_up)
    grad_two = lax.psum_scatter(
        (mult_nt(grad_gate, gate_full) + mult_nt(grad_up, up_full)).astype(jnp.bfloat16),
        "tensor",
        scatter_dimension=0,
        tiled=True,
    ).astype(jnp.float32)
    gain_two = jnp.sum(grad_two * normed_two, axis=0)
    grad_middle = grad_out + norm_back(grad_two * norm_ffn, normed_two, inverse_two)
    low_middle = grad_middle.astype(jnp.bfloat16)
    grad_attn_rows = lax.all_gather(low_middle, "tensor", axis=0, tiled=True)
    grad_out_w = mult_tn(attended, grad_attn_rows)
    grad_attended = (
        mult_nt(grad_attn_rows, out_full)
        .astype(jnp.bfloat16)
        .reshape(count, BLOCK, k_heads, group, head)
    )

    def backward_block(carry, item):
        grad_key, grad_value = carry
        qblock, dblock, lse_block, start = item
        scores, scale = block_scores(qblock, start, key_rot, segment)
        probs = jnp.exp(scores - lse_block[..., None])
        low_probs = probs.astype(jnp.bfloat16)
        grad_value = grad_value + jnp.einsum(
            "kgbs,bkgd->skd", low_probs, dblock, preferred_element_type=jnp.float32
        )
        grad_probs = jnp.einsum(
            "bkgd,skd->kgbs", dblock, value_rot, preferred_element_type=jnp.float32
        )
        grad_scores = probs * (grad_probs - jnp.sum(probs * grad_probs, axis=-1, keepdims=True))
        low_scores = (grad_scores * scale).astype(jnp.bfloat16)
        grad_query = jnp.einsum(
            "kgbs,skd->bkgd", low_scores, key_rot, preferred_element_type=jnp.float32
        )
        grad_key = grad_key + jnp.einsum(
            "kgbs,bkgd->skd", low_scores, qblock, preferred_element_type=jnp.float32
        )
        return ((grad_key, grad_value), grad_query)

    empty = jnp.zeros((rows, k_heads, head), jnp.float32)
    (grad_key, grad_value), grad_query = lax.scan(
        backward_block, (empty, empty), (query_blocks, grad_attended, lse, starts)
    )
    grad_query = grad_query.reshape(rows, q_heads, head)
    query_back = rotate_back(grad_query, cosine, sine)
    gain_query = jnp.sum(query_back * query_normed, axis=(0, 1))
    grad_query_raw = (
        norm_back(query_back * query_gain, query_normed, query_inverse)
        .astype(jnp.bfloat16)
        .reshape(rows, q_heads * head)
    )
    key_back = rotate_back(grad_key, cosine, sine)
    gain_key = jnp.sum(key_back * key_normed, axis=(0, 1))
    grad_key_raw = (
        norm_back(key_back * key_gain, key_normed, key_inverse)
        .astype(jnp.bfloat16)
        .reshape(rows, k_heads * head)
    )
    grad_value_low = grad_value.astype(jnp.bfloat16).reshape(rows, k_heads * head)
    grad_query_w = mult_tn(gathered_one, grad_query_raw)
    grad_key_w = mult_tn(gathered_one, grad_key_raw)
    grad_value_w = mult_tn(gathered_one, grad_value_low)
    grad_one_part = (
        mult_nt(grad_query_raw, query_full)
        + mult_nt(grad_key_raw, key_full)
        + mult_nt(grad_value_low, value_full)
    )
    grad_one = lax.psum_scatter(
        grad_one_part.astype(jnp.bfloat16), "tensor", scatter_dimension=0, tiled=True
    ).astype(jnp.float32)
    gain_one = jnp.sum(grad_one * normed_one, axis=0)
    grad_input = grad_middle + norm_back(grad_one * norm_attn, normed_one, inverse_one)
    gains = lax.psum((gain_one, gain_query, gain_key, gain_two), ("dp", "tensor"))
    attn_grads = (
        lax.psum_scatter(
            grad_query_w.astype(jnp.bfloat16), "dp", scatter_dimension=0, tiled=True
        ).astype(jnp.float32),
        lax.psum_scatter(
            grad_key_w.astype(jnp.bfloat16), "dp", scatter_dimension=0, tiled=True
        ).astype(jnp.float32),
        lax.psum_scatter(
            grad_value_w.astype(jnp.bfloat16), "dp", scatter_dimension=0, tiled=True
        ).astype(jnp.float32),
        lax.psum_scatter(
            grad_out_w.astype(jnp.bfloat16), "dp", scatter_dimension=1, tiled=True
        ).astype(jnp.float32),
    )
    ffn_grads = (
        lax.psum_scatter(
            grad_gate_w.astype(jnp.bfloat16), "dp", scatter_dimension=0, tiled=True
        ).astype(jnp.float32),
        lax.psum_scatter(
            grad_up_w.astype(jnp.bfloat16), "dp", scatter_dimension=0, tiled=True
        ).astype(jnp.float32),
        lax.psum_scatter(
            grad_down.astype(jnp.bfloat16), "dp", scatter_dimension=1, tiled=True
        ).astype(jnp.float32),
    )
    return (
        output,
        grad_input,
        gains[0],
        attn_grads[0],
        attn_grads[1],
        attn_grads[2],
        attn_grads[3],
        gains[1],
        gains[2],
        gains[3],
        ffn_grads[0],
        ffn_grads[1],
        ffn_grads[2],
    )


def solution(mesh):
    placed = (
        P(("dp", "tensor"), None),
        P("dp", None),
        P(),
        P("dp", "tensor"),
        P("dp", "tensor"),
        P("dp", "tensor"),
        P("tensor", "dp"),
        P(),
        P(),
        P(),
        P("dp", "tensor"),
        P("dp", "tensor"),
        P("tensor", "dp"),
        P(("dp", "tensor"), None),
    )
    return jax.shard_map(
        on_device,
        mesh=mesh,
        in_specs=placed,
        out_specs=(
            P(("dp", "tensor"), None),
            P(("dp", "tensor"), None),
            P(),
            P("dp", "tensor"),
            P("dp", "tensor"),
            P("dp", "tensor"),
            P("tensor", "dp"),
            P(),
            P(),
            P(),
            P("dp", "tensor"),
            P("dp", "tensor"),
            P("tensor", "dp"),
        ),
        check_vma=False,
    )
```

profile of v0, /device:TPU:1, one launch (start us, length us, event | category | flops | bytes accessed | tf_op | source)
XLA Modules:
  0.0 2169.8 jit_solution(10031025811667719515)
XLA Ops:
  12.7 71.5 %all_gather.35 = bf16[1024,128]{1,0:T(8,128)(2,1)S(1)} all-gather(bf16[32,128]{1,0:T(8,128)(2,1)} %param.18), channel_id=1, replica_groups=mesh['dp'=32,'tensor'=4] {'dp'}, dimensions={0}, use_global_device_ids=true | all-gather | bytes 270336 | tf_op jit(solution)/shard_map/all_gather | solution.py:119
  84.2 63.1 %all_gather.34 = bf16[1024,128]{1,0:T(8,128)(2,1)S(1)} all-gather(bf16[32,128]{1,0:T(8,128)(2,1)} %param.19), channel_id=1, replica_groups=mesh['dp'=32,'tensor'=4] {'dp'}, dimensions={0}, use_global_device_ids=true | all-gather | bytes 270336 | tf_op jit(solution)/shard_map/all_gather | solution.py:120
  147.9 66.1 %all_gather.36 = bf16[1024,256]{1,0:T(8,128)(2,1)S(1)} all-gather(bf16[32,256]{1,0:T(8,128)(2,1)} %param.17), channel_id=1, replica_groups=mesh['dp'=32,'tensor'=4] {'dp'}, dimensions={0}, use_global_device_ids=true | all-gather | bytes 540672 | tf_op jit(solution)/shard_map/all_gather | solution.py:118
  214.0 64.8 %all_gather.37 = bf16[256,1024]{0,1:T(8,128)(2,1)S(1)} all-gather(bf16[256,32]{0,1:T(8,128)(2,1)S(1)} %copy-done.28), channel_id=1, replica_groups=mesh['dp'=32,'tensor'=4] {'dp'}, dimensions={1}, use_global_device_ids=true | all-gather | bytes 540672 | tf_op jit(solution)/shard_map/all_gather | solution.py:121
  290.1 90.1 %reduce-scatter.12.cloned.1.call-done = f32[128,1024]{1,0:T(8,128)} async-done(((f32[512,1024]{1,0:T(8,128)}), f32[128,1024]{1,0:T(8,128)}) %reduce-scatter.12.cloned.1.call-update) | async-done | bytes 524304 | tf_op jit(solution)/shard_map/reduce_scatter | solution.py:148
  385.1 98.3 %all-gather.14.cloned.1.call-done = bf16[1024,1152]{1,0:T(8,128)(2,1)} async-done(((bf16[32,1152]{1,0:T(8,128)(2,1)}), bf16[1024,1152]{1,0:T(8,128)(2,1)}) %all-gather.14.cloned.1.call-update) | async-done | bytes 2359312 | tf_op jit(solution)/shard_map/all_gather | solution.py:152
  483.3 44.2 %all-gather.10.cloned.1.call-done = bf16[512,1024]{1,0:T(8,128)(2,1)} async-done(((bf16[128,1024]{1,0:T(8,128)(2,1)}), bf16[512,1024]{1,0:T(8,128)(2,1)}) %all-gather.10.cloned.1.call-update) | async-done | bytes 1048592 | tf_op jit(solution)/shard_map/all_gather | solution.py:157
  532.5 129.3 %all-gather.12.cloned.1.call-done = bf16[1024,1152]{1,0:T(8,128)(2,1)} async-done(((bf16[32,1152]{1,0:T(8,128)(2,1)}), bf16[1024,1152]{1,0:T(8,128)(2,1)}) %all-gather.12.cloned.1.call-update) | async-done | bytes 2359312 | tf_op jit(solution)/shard_map/all_gather | solution.py:151
  666.8 39.1 %all-gather.18.cloned.1.call-done = bf16[512,1024]{1,0:T(8,128)(2,1)} async-done(((bf16[128,1024]{1,0:T(8,128)(2,1)}), bf16[512,1024]{1,0:T(8,128)(2,1)}) %all-gather.18.cloned.1.call-update) | async-done | bytes 1048592 | tf_op jit(solution)/shard_map/all_gather | solution.py:168
  706.0 134.4 %all-gather.16.cloned.1.call-done = bf16[1152,1024]{0,1:T(8,128)(2,1)} async-done(((bf16[1152,32]{0,1:T(8,128)(2,1)}), bf16[1152,1024]{0,1:T(8,128)(2,1)}) %all-gather.16.cloned.1.call-update) | async-done | bytes 2359312 | tf_op jit(solution)/shard_map/all_gather | solution.py:153
  840.4 6.7 multiply_convert_fusion
  852.2 53.2 %reduce-scatter.16.cloned.1.call-done = bf16[128,1024]{1,0:T(8,128)(2,1)} async-done(((bf16[512,1024]{1,0:T(8,128)(2,1)}), bf16[128,1024]{1,0:T(8,128)(2,1)}) %reduce-scatter.16.cloned.1.call-update) | async-done | bytes 262160 | tf_op jit(solution)/shard_map/reduce_scatter | solution.py:175
  913.6 16.9 all-gather.20.cloned.1.call-done
  938.0 8.7 fusion.18
  954.8 8.7 fusion.12
  990.0 81.2 %reduce-scatter.24.cloned.1.call-done = bf16[32,128]{1,0:T(8,128)(2,1)} async-done(((bf16[1024,128]{1,0:T(8,128)(2,1)}), bf16[32,128]{1,0:T(8,128)(2,1)}) %reduce-scatter.24.cloned.1.call-update) | async-done | bytes 8208 | tf_op jit(solution)/shard_map/reduce_scatter | solution.py:255
  1072.5 157.8 %reduce-scatter.22.cloned.1.call-done = bf16[32,128]{1,0:T(8,128)(2,1)} async-done(((bf16[1024,128]{1,0:T(8,128)(2,1)}), bf16[32,128]{1,0:T(8,128)(2,1)}) %reduce-scatter.22.cloned.1.call-update) | async-done | bytes 8208 | tf_op jit(solution)/shard_map/reduce_scatter | solution.py:252
  1231.6 157.2 %reduce-scatter.26.cloned.1.call-done = bf16[256,32]{0,1:T(8,128)(2,1)} async-done(((bf16[256,1024]{0,1:T(8,128)(2,1)}), bf16[256,32]{0,1:T(8,128)(2,1)}) %reduce-scatter.26.cloned.1.call-update) | async-done | bytes 16400 | tf_op jit(solution)/shard_map/reduce_scatter | solution.py:258
  1390.2 158.0 %reduce-scatter.20.cloned.1.call-done = bf16[32,256]{1,0:T(8,128)(2,1)} async-done(((bf16[1024,256]{1,0:T(8,128)(2,1)}), bf16[32,256]{1,0:T(8,128)(2,1)}) %reduce-scatter.20.cloned.1.call-update) | async-done | bytes 16400 | tf_op jit(solution)/shard_map/reduce_scatter | solution.py:249
  1549.5 163.0 %reduce-scatter.30.cloned.1.call-done = bf16[32,1152]{1,0:T(8,128)(2,1)} async-done(((bf16[1024,1152]{1,0:T(8,128)(2,1)}), bf16[32,1152]{1,0:T(8,128)(2,1)}) %reduce-scatter.30.cloned.1.call-update) | async-done | bytes 73744 | tf_op jit(solution)/shard_map/reduce_scatter | solution.py:266
  1714.1 161.1 %reduce-scatter.28.cloned.1.call-done = bf16[32,1152]{1,0:T(8,128)(2,1)} async-done(((bf16[1024,1152]{1,0:T(8,128)(2,1)}), bf16[32,1152]{1,0:T(8,128)(2,1)}) %reduce-scatter.28.cloned.1.call-update) | async-done | bytes 73744 | tf_op jit(solution)/shard_map/reduce_scatter | solution.py:263
  1876.8 161.3 %reduce-scatter.32.cloned.1.call-done = bf16[1152,32]{0,1:T(8,128)(2,1)} async-done(((bf16[1152,1024]{0,1:T(8,128)(2,1)}), bf16[1152,32]{0,1:T(8,128)(2,1)}) %reduce-scatter.32.cloned.1.call-update) | async-done | bytes 73744 | tf_op jit(solution)/shard_map/reduce_scatter | solution.py:269
  2039.7 53.2 %reduce-scatter.18.cloned.1.call-done = bf16[128,1024]{1,0:T(8,128)(2,1)} async-done(((bf16[512,1024]{1,0:T(8,128)(2,1)}), bf16[128,1024]{1,0:T(8,128)(2,1)}) %reduce-scatter.18.cloned.1.call-update) | async-done | bytes 262160 | tf_op jit(solution)/shard_map/reduce_scatter | solution.py:242
  2094.1 66.2 %all-reduce = (f32[1024]{0:T(1024)}, f32[64]{0:T(128)}, f32[64]{0:T(128)}, f32[1024]{0:T(1024)}) all-reduce(f32[1024]{0:T(1024)S(1)} %get-tuple-element.56, f32[64]{0:T(128)S(1)} %reduce_sum.175, f32[64]{0:T(128)S(1)} %reduce_sum.178, f32[1024]{0:T(1024)S(1)} %copy-done.27), channel_id=1, replica_groups=mesh['dp'=32,'tensor'=4] {'dp','tensor'}, use_global_device_ids=true, to_apply=%region_19.20 | all-reduce | flops 2176 | bytes 17408 | tf_op jit(solution)/shard_map/psum | solution.py:247
  (205 shorter events, 99.4 us)
Async XLA Ops:
  8.0 270.7 %all-gather.8.cloned.1.call-start = ((), (), s32[]{:S(2)}) async-start(), calls=%async_computation.11 | async-start | bytes 1310720 | tf_op jit(solution)/shard_map/all_gather | solution.py:125
  11.0 369.2 %reduce-scatter.12.cloned.1.call-start = ((), (), s32[]{:S(2)}) async-start(), calls=%async_computation.12 | async-start | bytes 2621440 | tf_op jit(solution)/shard_map/reduce_scatter | solution.py:148
  289.5 193.9 %all-gather.14.cloned.1.call-start = ((), (), s32[]{:S(2)}) async-start(), calls=%async_computation.15 | async-start | bytes 2433024 | tf_op jit(solution)/shard_map/all_gather | solution.py:152
  290.1 237.5 %all-gather.10.cloned.1.call-start = ((), (), s32[]{:S(2)}) async-start(), calls=%async_computation.13 | async-start | bytes 1310720 | tf_op jit(solution)/shard_map/all_gather | solution.py:157
  382.8 279.1 %all-gather.12.cloned.1.call-start = ((), (), s32[]{:S(2)}) async-start(), calls=%async_computation.14 | async-start | bytes 2433024 | tf_op jit(solution)/shard_map/all_gather | solution.py:151
  383.4 322.6 %all-gather.18.cloned.1.call-start = ((), (), s32[]{:S(2)}) async-start(), calls=%async_computation.18 | async-start | bytes 1310720 | tf_op jit(solution)/shard_map/all_gather | solution.py:168
  384.1 456.3 %all-gather.16.cloned.1.call-start = ((), (), s32[]{:S(2)}) async-start(), calls=%async_computation.16 | async-start | bytes 2433024 | tf_op jit(solution)/shard_map/all_gather | solution.py:153
  384.8 520.5 %reduce-scatter.16.cloned.1.call-start = ((), (), s32[]{:S(2)}) async-start(), calls=%async_computation.19 | async-start | bytes 1310720 | tf_op jit(solution)/shard_map/reduce_scatter | solution.py:175
  852.1 78.3 %all-gather.20.cloned.1.call-start = ((), (), s32[]{:S(2)}) async-start(), calls=%async_computation.20 | async-start | bytes 1310720 | tf_op jit(solution)/shard_map/all_gather | solution.py:184
  909.7 161.5 %reduce-scatter.24.cloned.1.call-start = ((), (), s32[]{:S(2)}) async-start(), calls=%async_computation.24 | async-start | bytes 270336 | tf_op jit(solution)/shard_map/reduce_scatter | solution.py:255
  938.0 292.4 %reduce-scatter.22.cloned.1.call-start = ((), (), s32[]{:S(2)}) async-start(), calls=%async_computation.23 | async-start | bytes 270336 | tf_op jit(solution)/shard_map/reduce_scatter | solution.py:252
  951.0 437.9 %reduce-scatter.26.cloned.1.call-start = ((), (), s32[]{:S(2)}) async-start(), calls=%async_computation.25 | async-start | bytes 540672 | tf_op jit(solution)/shard_map/reduce_scatter | solution.py:258
  954.7 593.5 %reduce-scatter.20.cloned.1.call-start = ((), (), s32[]{:S(2)}) async-start(), calls=%async_computation.22 | async-start | bytes 540672 | tf_op jit(solution)/shard_map/reduce_scatter | solution.py:249
  966.3 746.2 %reduce-scatter.30.cloned.1.call-start = ((), (), s32[]{:S(2)}) async-start(), calls=%async_computation.27 | async-start | bytes 2433024 | tf_op jit(solution)/shard_map/reduce_scatter | solution.py:266
  971.0 904.2 %reduce-scatter.28.cloned.1.call-start = ((), (), s32[]{:S(2)}) async-start(), calls=%async_computation.26 | async-start | bytes 2433024 | tf_op jit(solution)/shard_map/reduce_scatter | solution.py:263
  976.5 1061.6 %reduce-scatter.32.cloned.1.call-start = ((), (), s32[]{:S(2)}) async-start(), calls=%async_computation.28 | async-start | bytes 2433024 | tf_op jit(solution)/shard_map/reduce_scatter | solution.py:269
  982.0 1110.8 %reduce-scatter.18.cloned.1.call-start = ((), (), s32[]{:S(2)}) async-start(), calls=%async_computation.21 | async-start | bytes 1310720 | tf_op jit(solution)/shard_map/reduce_scatter | solution.py:242
  985.4 1107.4 %copy-start.22 = (f32[1024]{0:T(1024)S(1)}, f32[1024]{0:T(1024)}, u32[]{:S(2)}) copy-start(f32[1024]{0:T(1024)} %param.16) | copy-start | bytes 12292
  985.4 1107.4 %copy-start.34 = (f32[128]{0:T(128)S(1)}, f32[128]{0:T(128)}, u32[]{:S(2)}) copy-start(f32[128]{0:T(128)} %copy-done.33) | copy-start | bytes 1540
  985.5 1174.8 %reduce-scatter.14.cloned.1.call-start = ((), (), s32[]{:S(2)}) async-start(), calls=%async_computation.17 | async-start | bytes 1310720 | tf_op jit(solution)/shard_map/reduce_scatter | solution.py:163
  989.7 1170.5 %copy-start.6 = (bf16[128,1024]{1,0:T(8,128)(2,1)S(1)}, bf16[128,1024]{1,0:T(8,128)(2,1)}, u32[]{:S(2)}) copy-start(bf16[128,1024]{1,0:T(8,128)(2,1)} %param.27) | copy-start | bytes 786436
  989.7 1170.5 %copy-start.11 = (bf16[128,1024]{1,0:T(8,128)(2,1)S(1)}, bf16[128,1024]{1,0:T(8,128)(2,1)}, u32[]{:S(2)}) copy-start(bf16[128,1024]{1,0:T(8,128)(2,1)} %reduce-scatter.16.cloned.1.call-done) | copy-start | bytes 786436
  989.7 1170.5 %copy-start.30 = (f32[128]{0:T(128)S(1)}, f32[128]{0:T(128)}, u32[]{:S(2)}) copy-start(f32[128]{0:T(128)} %copy-done.29) | copy-start | bytes 1540
  989.7 1170.5 %copy-start.36 = (f32[128]{0:T(128)S(1)}, f32[128]{0:T(128)}, u32[]{:S(2)}) copy-start(f32[128]{0:T(128)} %copy-done.35) | copy-start | bytes 1540
  (40 other events, 2130.3 us)
Sparse Core Ops, SparseCore 0:
  11.1 24.5 all-gather.7
  289.6 90.5 reduce-scatter.11
  852.2 53.0 reduce-scatter.15
  909.8 20.5 all-gather.19
Sparse Core Ops, SparseCore 1:
  291.6 191.7 all-gather.13
  485.6 42.0 all-gather.9
  529.2 132.6 all-gather.11
  663.6 42.3 all-gather.17
  707.7 132.6 all-gather.15
  938.0 133.1 reduce-scatter.23
  1074.1 156.1 reduce-scatter.21
  1232.5 156.3 reduce-scatter.25
  1391.8 156.3 reduce-scatter.19
  1550.6 161.9 reduce-scatter.29
  1714.8 160.3 reduce-scatter.27
  1877.6 160.4 reduce-scatter.31
  2040.6 52.2 reduce-scatter.17
  2095.7 31.2 reduce-scatter.13
where the time goes:
time: 2170 us
  waiting for transfers between devices  1700 us (78%)
  blocking collectives  332 us (15%)
  matrix products  78 us (4%)
  other arithmetic  31 us (1%)
    reduce_scatter x1, waiting for transfers between devices, on_device(): lax.psum_scatter(grad_up_w.astype(jnp.bfloat16), 'dp', scatter_dimension=...  163 us
    reduce_scatter x1, waiting for transfers between devices, on_device(): lax.psum_scatter(grad_down.astype(jnp.bfloat16), 'dp', scatter_dimension=...  161 us
    reduce_scatter x1, waiting for transfers between devices, on_device(): lax.psum_scatter(grad_gate_w.astype(jnp.bfloat16), 'dp', scatter_dimensio...  161 us
    reduce_scatter x1, waiting for transfers between devices, on_device(): lax.psum_scatter(grad_query_w.astype(jnp.bfloat16), 'dp', scatter_dimensi...  158 us
    reduce_scatter x1, waiting for transfers between devices, on_device(): lax.psum_scatter(grad_key_w.astype(jnp.bfloat16), 'dp', scatter_dimension...  158 us
    reduce_scatter x1, waiting for transfers between devices, on_device(): lax.psum_scatter(grad_out_w.astype(jnp.bfloat16), 'dp', scatter_dimension...  157 us
    all_gather x1, waiting for transfers between devices, on_device(): lax.all_gather(w_down, 'dp', axis=1, tiled=True)  134 us
    all_gather x1, waiting for transfers between devices, on_device(): lax.all_gather(w_gate, 'dp', axis=0, tiled=True)  129 us
  transfers between devices with their start and end apart: 18, of which 16 were waited for; matrix products, arithmetic and copies ran while one was open for 4% of the time, Pallas kernels for 0%

commit v1 on v0

v1 whole, which is shorter than its diff:
```python
import functools
import math

import jax
import jax.numpy as jnp
import numpy as np
from jax import lax
from jax.experimental import pallas as pl
from jax.experimental.pallas import tpu as pltpu
from jax.sharding import PartitionSpec as P

MESH = pl.DeviceIdType.MESH
BF = jnp.bfloat16
F32 = jnp.float32

D = 1024
HD = 64
FF_PARTS = (384, 384, 384)
FF_OFF = tuple(int(v) for v in np.cumsum((0,) + FF_PARTS)[:-1])
WIDTHS = (768,) + tuple(3 * c for c in FF_PARTS)
CHUNKS = len(WIDTHS)
FFL = sum(FF_PARTS)
EPS = 1e-05
THETA = 1000000.0
GAINS = 2304
NSEM = 34 * CHUNKS + 40

LO = pl.ds(0, 16)
HI = pl.ds(16, 16)


def dot(a, b):
    return jnp.dot(a, b, preferred_element_type=F32)


def dot_nt(a, b):
    return lax.dot_general(a, b, (((1,), (1,)), ((), ())), preferred_element_type=F32)


def dot_tn(a, b):
    return lax.dot_general(a, b, (((0,), (0,)), ((), ())), preferred_element_type=F32)


def rms(v):
    inverse = lax.rsqrt(jnp.mean(v * v, axis=-1, keepdims=True) + EPS)
    return v * inverse, inverse


def kernel(
    lens, tok, cot, wq, wk, wv, wo, wg, wu, wd, na, nf, qg, kg, fr,
    out, gtok, gq_w, gk_w, gv_w, go_w, gg_w, gu_w, gd_w, gains,
    Ws, Gs, RA, RB, RC, RD, RE,
    A1, A2, GO, GX, A1T, A2T, GOT,
    PB, T1, T2, X2, DX2,
    COS, SIN, BIAS, NQ, RQ, QS, KD, VD, PR, O, DO, DQ, DK, DV, DQKV,
    HID, DG, DU, DA, GV,
    ssem, rsem,
):
    me = lax.axis_index("dp")
    t = lax.axis_index("tensor")
    x = me // 16
    z = (me // 4) % 4
    y = me % 4
    xo = (x + 1) % 2
    zl, zr, zo = (z + 3) % 4, (z + 1) % 4, (z + 2) % 4
    yl, yr, yo = (y + 3) % 4, (y + 1) % 4, (y + 2) % 4
    ts = t + 1 - 2 * (t % 2)
    to = (t + 2) % 4
    td = (ts + 2) % 4

    def dp(xx, zz, yy):
        return (xx * 16 + zz * 4 + yy, t)

    d_x = dp(xo, z, y)
    d_zl, d_zr, d_zo = dp(x, zl, y), dp(x, zr, y), dp(x, zo, y)
    d_yl, d_yr, d_yo = dp(x, z, yl), dp(x, z, yr), dp(x, z, yo)
    d_s, d_o, d_d = (me, ts), (me, to), (me, td)
    partners = (d_x, d_zl, d_zr, d_zo, d_yl, d_yr, d_yo, d_s, d_o, d_d)

    started = []

    def send(src, dst, device):
        index = len(started)
        copy = pltpu.make_async_remote_copy(
            src_ref=src,
            dst_ref=dst,
            send_sem=ssem.at[index],
            recv_sem=rsem.at[index],
            device_id=device,
            device_id_type=MESH,
        )
        copy.start()
        started.append(copy)
        return copy

    ag = {}

    def ag0(c):
        W = Ws[c]
        ag[c, 0] = send(W.at[x, z, y], W.at[x, z, y], d_x)

    def ag1(c):
        W = Ws[c]
        ag[c, 0].wait_recv()
        a, b = W.at[:, z, y, LO], W.at[:, z, y, HI]
        ag[c, 1] = (send(a, a, d_zr), send(a, a, d_zl), send(b, b, d_yr), send(b, b, d_yl))

    def ag2(c):
        W, r = Ws[c], ag[c, 1]
        r[0].wait_recv()
        v = W.at[0, zl, y, LO]
        f0 = send(v, v, d_zr)
        r[2].wait_recv()
        v = W.at[0, z, yl, HI]
        f2 = send(v, v, d_yr)
        r[1].wait_recv()
        v = W.at[1, zr, y, LO]
        f1 = send(v, v, d_zl)
        r[3].wait_recv()
        v = W.at[1, z, yr, HI]
        f3 = send(v, v, d_yl)
        ag[c, 2] = (f0, f1, f2, f3)

    def ag3(c):
        W, r = Ws[c], ag[c, 2]
        r[0].wait_recv()
        r[1].wait_recv()
        a = W.at[:, :, y, LO]
        f0, f1 = send(a, a, d_yr), send(a, a, d_yl)
        r[2].wait_recv()
        r[3].wait_recv()
        b = W.at[:, z, :, HI]
        ag[c, 3] = (f0, f1, send(b, b, d_zr), send(b, b, d_zl))

    def ag4(c):
        W, r = Ws[c], ag[c, 3]
        r[0].wait_recv()
        v = W.at[0, :, yl, LO]
        f0 = send(v, v, d_yr)
        r[2].wait_recv()
        v = W.at[0, zl, :, HI]
        f2 = send(v, v, d_zr)
        r[1].wait_recv()
        v = W.at[1, :, yr, LO]
        f1 = send(v, v, d_yl)
        r[3].wait_recv()
        v = W.at[1, zr, :, HI]
        f3 = send(v, v, d_zl)
        ag[c, 4] = (f0, f1, f2, f3)

    def ag5(c):
        for copy in ag[c, 4]:
            copy.wait_recv()

    ag_steps = (ag0, ag1, ag2, ag3, ag4, ag5)

    rs = {}

    def add(ref, index, *others):
        total = ref[index].astype(F32)
        for other in others:
            total = total + other.astype(F32).reshape(total.shape)
        ref[index] = total.astype(BF)

    lo, hi = slice(0, 16), slice(16, 32)
    every = slice(None)

    def one(i):
        return pl.ds(i, 1)

    def rs1(c):
        G, ra = Gs[c], RA[c]
        rs[c, 1] = (
            send(G.at[0, :, yo, LO], ra.at[0, 0], d_yr),
            send(G.at[1, :, yo, LO], ra.at[0, 1], d_yl),
            send(G.at[0, zo, :, HI], ra.at[1, 0], d_zr),
            send(G.at[1, zo, :, HI], ra.at[1, 1], d_zl),
        )

    def rs2(c):
        G, ra, rb, r = Gs[c], RA[c], RB[c], rs[c, 1]
        r[0].wait_recv()
        add(G, (0, every, one(yr), lo), ra[0, 0])
        f0 = send(G.at[:, :, yr, LO], rb.at[0, 0], d_yr)
        r[2].wait_recv()
        add(G, (0, one(zr), every, hi), ra[1, 0])
        f2 = send(G.at[:, zr, :, HI], rb.at[1, 0], d_zr)
        r[1].wait_recv()
        add(G, (1, every, one(yl), lo), ra[0, 1])
        f1 = send(G.at[:, :, yl, LO], rb.at[0, 1], d_yl)
        r[3].wait_recv()
        add(G, (1, one(zl), every, hi), ra[1, 1])
        f3 = send(G.at[:, zl, :, HI], rb.at[1, 1], d_zl)
        rs[c, 2] = (f0, f1, f2, f3)

    def rs3(c):
        G, rb, rc, r = Gs[c], RB[c], RC[c], rs[c, 2]
        r[0].wait_recv()
        r[1].wait_recv()
        add(G, (every, every, one(y), lo), rb[0, 0], rb[0, 1])
        f0 = send(G.at[0, zo, y, LO], rc.at[0, 0], d_zr)
        f1 = send(G.at[1, zo, y, LO], rc.at[0, 1], d_zl)
        r[2].wait_recv()
        r[3].wait_recv()
        add(G, (every, one(z), every, hi), rb[1, 0], rb[1, 1])
        f2 = send(G.at[0, z, yo, HI], rc.at[1, 0], d_yr)
        f3 = send(G.at[1, z, yo, HI], rc.at[1, 1], d_yl)
        rs[c, 3] = (f0, f1, f2, f3)

    def rs4(c):
        G, rc, rd, r = Gs[c], RC[c], RD[c], rs[c, 3]
        r[0].wait_recv()
        add(G, (0, one(zr), one(y), lo), rc[0, 0])
        f0 = send(G.at[:, zr, y, LO], rd.at[0, 0], d_zr)
        r[2].wait_recv()
        add(G, (0, one(z), one(yr), hi), rc[1, 0])
        f2 = send(G.at[:, z, yr, HI], rd.at[1, 0], d_yr)
        r[1].wait_recv()
        add(G, (1, one(zl), one(y), lo), rc[0, 1])
        f1 = send(G.at[:, zl, y, LO], rd.at[0, 1], d_zl)
        r[3].wait_recv()
        add(G, (1, one(z), one(yl), hi), rc[1, 1])
        f3 = send(G.at[:, z, yl, HI], rd.at[1, 1], d_yl)
        rs[c, 4] = (f0, f1, f2, f3)

    def rs5(c):
        G, rd, r = Gs[c], RD[c], rs[c, 4]
        for copy in r:
            copy.wait_recv()
        add(G, (every, one(z), one(y), lo), rd[0, 0], rd[0, 1])
        add(G, (every, one(z), one(y), hi), rd[1, 0], rd[1, 1])
        rs[c, 5] = send(G.at[xo, z, y], RE[c], d_x)

    def rs6(c):
        rs[c, 5].wait_recv()
        total = Gs[c][x, z, y].astype(F32) + RE[c][...].astype(F32)
        if c == 0:
            gq_w[...] = total[:, 0:256]
            gk_w[...] = total[:, 256:384]
            gv_w[...] = total[:, 384:512]
            go_w[...] = total[:, 512:768]
        else:
            w, o = FF_PARTS[c - 1], FF_OFF[c - 1]
            gg_w[:, o : o + w] = total[:, 0:w]
            gu_w[:, o : o + w] = total[:, w : 2 * w]
            gd_w[:, o : o + w] = total[:, 2 * w : 3 * w]

    rs_steps = (None, rs1, rs2, rs3, rs4, rs5, rs6)

    def rows_start(buf):
        v = buf.at[t]
        return send(v, v, d_o), send(v, v, d_s)

    def rows_relay(buf, pair):
        pair[0].wait_recv()
        v = buf.at[to]
        return send(v, v, d_s)

    def rows_end(pair, relay):
        pair[1].wait_recv()
        relay.wait_recv()

    def sum_start(k, part):
        PB[k, td] = part(td)
        c0 = send(PB.at[k, td], T1.at[k, 1], d_s)
        PB[k, ts] = part(ts)
        c1 = send(PB.at[k, ts], T1.at[k, 0], d_s)
        PB[k, to] = part(to)
        PB[k, t] = part(t)
        return c0, c1

    def sum_mid(k, copies):
        copies[0].wait_recv()
        PB[k, to] = (PB[k, to].astype(F32) + T1[k, 1].astype(F32)).astype(BF)
        return send(PB.at[k, to], T2.at[k], d_o)

    def sum_end(k, copies, last):
        copies[1].wait_recv()
        part = PB[k, t].astype(F32) + T1[k, 0].astype(F32)
        last.wait_recv()
        return part + T2[k].astype(F32)

    barrier = pltpu.get_barrier_semaphore()
    for device in partners:
        pl.semaphore_signal(barrier, inc=1, device_id=device, device_id_type=MESH)

    W0 = Ws[0]
    W0[x, z, y, :, 0:256] = wq[...]
    W0[x, z, y, :, 256:384] = wk[...]
    W0[x, z, y, :, 384:512] = wv[...]
    W0[x, z, y, :, 512:768] = wo[...]
    for c in range(1, CHUNKS):
        w, o = FF_PARTS[c - 1], FF_OFF[c - 1]
        Ws[c][x, z, y, :, 0:w] = wg[:, o : o + w]
        Ws[c][x, z, y, :, w : 2 * w] = wu[:, o : o + w]
        Ws[c][x, z, y, :, 2 * w : 3 * w] = wd[:, o : o + w]
    n1, _ = rms(tok[...].astype(F32))
    A1[t] = (n1 * na[...]).astype(BF)
    GO[t] = cot[...]

    pl.semaphore_wait(barrier, len(partners))

    ag0(0)
    a1_pair = rows_start(A1)
    for c in range(1, CHUNKS):
        ag0(c)

    lane = lax.broadcasted_iota(jnp.int32, (1, 128), 1)
    left_head = lane < 64
    first_half = (lane % 64) < 32

    e1 = lens[0, 0]
    e2 = e1 + lens[0, 1]
    e3 = e2 + lens[0, 2]

    def begin(row):
        return jnp.where(
            row >= e3, e3, jnp.where(row >= e2, e2, jnp.where(row >= e1, e1, 0))
        )

    def fill_tables(i, carry):
        rows = pl.ds(pl.multiple_of(i * 128, 128), 128)
        row = lax.broadcasted_iota(jnp.int32, (128, 128), 0) + i * 128
        angle = (row - begin(row)).astype(F32) * fr[...]
        COS[rows] = jnp.cos(angle)
        SIN[rows] = jnp.where(first_half, -1.0, 1.0) * jnp.sin(angle)
        return carry

    def fill_bias(i, carry):
        rows = pl.ds(pl.multiple_of(i * 128, 128), 128)
        row = lax.broadcasted_iota(jnp.int32, (128, 512), 0) + i * 128
        col = lax.broadcasted_iota(jnp.int32, (128, 512), 1)
        seen = (col <= row) & (col >= begin(row))
        BIAS[rows] = jnp.where(seen, 0.0, -1e30)
        return carry

    ag1(0)
    lax.fori_loop(0, 4, fill_tables, 0)
    a1_relay = rows_relay(A1, a1_pair)
    ag2(0)
    go_pair = rows_start(GO)
    ag1(1)
    lax.fori_loop(0, 4, fill_bias, 0)
    ag3(0)
    rows_end(a1_pair, a1_relay)
    ag2(1)
    A1T[...] = A1[...].reshape(512, D).T
    go_relay = rows_relay(GO, go_pair)
    for c in range(2, CHUNKS):
        ag1(c)
    ag4(0)
    ag3(1)
    rows_end(go_pair, go_relay)
    GOT[...] = GO[...].reshape(512, D).T
    ag5(0)

    def rope(v, rows):
        swapped = jnp.where(first_half, pltpu.roll(v, 96, 1), pltpu.roll(v, 32, 1))
        return v * COS[rows] + swapped * SIN[rows]

    def rope_back(v, rows):
        swapped = jnp.where(first_half, pltpu.roll(v, 96, 1), pltpu.roll(v, 32, 1))
        return v * COS[rows] - swapped * SIN[rows]

    hr = lax.broadcasted_iota(jnp.int32, (128, 128), 0) // 64
    hc = lax.broadcasted_iota(jnp.int32, (128, 128), 1) // 64
    mean_of = jnp.where(hr == hc, 1.0 / HD, 0.0).astype(BF)

    def head_mean(v):
        high = v.astype(BF)
        low = (v - high.astype(F32)).astype(BF)
        return dot(high, mean_of) + dot(low, mean_of)

    q_gain = jnp.concatenate([qg[...], qg[...]], axis=1)
    k_gain = jnp.concatenate([kg[...], kg[...]], axis=1)

    def qkv_block(i, carry):
        rows = pl.ds(pl.multiple_of(i * 256, 256), 256)
        raw = dot(A1[pl.ds(2 * i, 2)].reshape(256, D), W0[:, :, :, :, 0:512].reshape(D, 512))
        for g in range(3):
            v = raw[:, 128 * g : 128 * g + 128]
            inverse = lax.rsqrt(head_mean(v * v) + EPS)
            n = v * inverse
            NQ[g, rows] = n
            RQ[g, rows] = inverse
            r = rope(n * (q_gain if g < 2 else k_gain), rows)
            if g < 2:
                QS[g, rows] = (r * HD**-0.5).astype(BF)
            else:
                turned = pltpu.roll(r, 64, 1)
                KD[0, rows] = jnp.where(left_head, r, turned).astype(BF)
                KD[1, rows] = jnp.where(left_head, turned, r).astype(BF)
        v = raw[:, 384:512]
        turned = pltpu.roll(v, 64, 1)
        VD[0, rows] = jnp.where(left_head, v, turned).astype(BF)
        VD[1, rows] = jnp.where(left_head, turned, v).astype(BF)
        return carry

    lax.fori_loop(0, 2, qkv_block, 0)

    def stack(v):
        none = jnp.zeros_like(v)
        return jnp.concatenate(
            [jnp.where(left_head, v, none), jnp.where(left_head, none, v)], axis=0
        )

    def unstack(v):
        half = v.shape[0] // 2
        return jnp.where(left_head, v[:half], v[half:])

    def attend(g, b):
        rows, keys = pl.ds(256 * b, 256), 256 * (b + 1)
        scores = dot_nt(stack(QS[g, rows]), KD[g, 0:keys])
        bias = BIAS[rows, 0:keys]
        scores = scores + jnp.concatenate([bias, bias], axis=0)
        expo = jnp.exp(scores - jnp.max(scores, axis=-1, keepdims=True))
        probs = expo * (1.0 / jnp.sum(expo, axis=-1, keepdims=True))
        PR[g, 512 * b : 512 * b + 512, 0:keys] = probs
        O[rows, 128 * g : 128 * g + 128] = unstack(dot(probs.astype(BF), VD[g, 0:keys])).astype(BF)

    ag4(1)
    attend(0, 0)
    attend(0, 1)
    ag2(2)
    attend(1, 0)
    attend(1, 1)
    ag3(2)

    def out_part(b):
        rows = pl.ds(pl.multiple_of(b * 128, 128), 128)
        return dot_nt(O[rows], W0[:, :, :, :, 512:768].reshape(D, 256)).astype(BF)

    at_copies = sum_start(0, out_part)
    for c in range(3, CHUNKS):
        ag2(c)
    at_last = sum_mid(0, at_copies)
    ag4(2)
    for c in range(3, CHUNKS):
        ag3(c)
    x2 = tok[...].astype(F32) + sum_end(0, at_copies, at_last)
    X2[...] = x2
    n2, _ = rms(x2)
    A2[t] = (n2 * nf[...]).astype(BF)
    a2_pair = rows_start(A2)
    ag5(1)
    for c in range(3, CHUNKS):
        ag4(c)
    a2_relay = rows_relay(A2, a2_pair)
    rows_end(a2_pair, a2_relay)
    A2T[...] = A2[...].reshape(512, D).T

    def ffn_chunk(c):
        W, G = Ws[c], Gs[c]
        w, o = FF_PARTS[c - 1], FF_OFF[c - 1]
        cols = slice(o, o + w)

        def block(i, carry):
            rows = pl.ds(pl.multiple_of(i * 256, 256), 256)
            a = A2[pl.ds(2 * i, 2)].reshape(256, D)
            g = GO[pl.ds(2 * i, 2)].reshape(256, D)
            gate = dot(a, W[:, :, :, :, 0:w].reshape(D, w))
            up = dot(a, W[:, :, :, :, w : 2 * w].reshape(D, w))
            dhid = dot(g, W[:, :, :, :, 2 * w : 3 * w].reshape(D, w))
            sigma = jax.nn.sigmoid(gate)
            swish = gate * sigma
            HID[rows, cols] = (swish * up).astype(BF)
            dgate = (dhid * up * sigma * (1.0 + gate * (1.0 - sigma))).astype(BF)
            dup = (dhid * swish).astype(BF)
            DG[rows, cols] = dgate
            DU[rows, cols] = dup
            part = dot_nt(dgate, W[:, :, :, :, 0:w].reshape(D, w)) + dot_nt(
                dup, W[:, :, :, :, w : 2 * w].reshape(D, w)
            )
            if c == 1:
                DA[rows] = part
            else:
                DA[rows] = DA[rows] + part
            return carry

        lax.fori_loop(0, 2, block, 0)

    def ffn_grads(c):
        G = Gs[c]
        w, o = FF_PARTS[c - 1], FF_OFF[c - 1]
        cols = slice(o, o + w)

        def block(i, carry):
            rows = pl.ds(pl.multiple_of(i * 256, 256), 256)
            zs = pl.ds(2 * (i % 2), 2)
            a, g = A2T[rows], GOT[rows]
            G[i // 2, zs, :, :, 0:w] = dot(a, DG[:, cols]).astype(BF).reshape(2, 4, 32, w)
            G[i // 2, zs, :, :, w : 2 * w] = dot(a, DU[:, cols]).astype(BF).reshape(2, 4, 32, w)
            G[i // 2, zs, :, :, 2 * w : 3 * w] = dot(g, HID[:, cols]).astype(BF).reshape(2, 4, 32, w)
            return carry

        lax.fori_loop(0, 4, block, 0)

    for c in range(1, CHUNKS):
        if c > 1:
            ag5(c)
        ffn_chunk(c)
        if c + 1 < CHUNKS:
            ffn_grads(c)
            rs1(c)
            if c > 1:
                rs2(c - 1)

    def da2_part(b):
        rows = pl.ds(pl.multiple_of(b * 128, 128), 128)
        return DA[rows].astype(BF)

    da2_copies = sum_start(1, da2_part)
    ffn_grads(CHUNKS - 1)
    rs1(CHUNKS - 1)
    da2_last = sum_mid(1, da2_copies)
    if CHUNKS > 2:
        rs2(CHUNKS - 2)

    def y_part(b):
        rows = pl.ds(pl.multiple_of(b * 128, 128), 128)
        total = None
        for c in range(1, CHUNKS):
            w, o = FF_PARTS[c - 1], FF_OFF[c - 1]
            part = dot_nt(HID[rows, o : o + w], Ws[c][:, :, :, :, 2 * w : 3 * w].reshape(D, w))
            total = part if total is None else total + part
        return total.astype(BF)

    y_copies = sum_start(2, y_part)

    da2 = sum_end(1, da2_copies, da2_last)
    n2, r2 = rms(X2[...])
    GV[0, pl.ds(t, 1), :, 1024:2048] = jnp.sum(da2 * n2, axis=0, keepdims=True).reshape(1, 1, D)
    h = da2 * nf[...]
    dx2 = cot[...].astype(F32) + r2 * (h - n2 * jnp.mean(h * n2, axis=-1, keepdims=True))
    DX2[...] = dx2
    GX[t] = dx2.astype(BF)
    gx_pair = rows_start(GX)
    rs2(CHUNKS - 1)
    gx_relay = rows_relay(GX, gx_pair)
    y_last = sum_mid(2, y_copies)
    if CHUNKS > 2:
        rs3(1)
    rows_end(gx_pair, gx_relay)

    def do_block(i, carry):
        rows = pl.ds(pl.multiple_of(i * 256, 256), 256)
        g = GX[pl.ds(2 * i, 2)].reshape(256, D)
        DO[rows] = dot(g, W0[:, :, :, :, 512:768].reshape(D, 256)).astype(BF)
        return carry

    lax.fori_loop(0, 2, do_block, 0)

    def attend_back(g, b):
        rows, keys = pl.ds(256 * b, 256), 256 * (b + 1)
        qs = stack(QS[g, rows])
        dos = stack(DO[rows, 128 * g : 128 * g + 128])
        probs = PR[g, 512 * b : 512 * b + 512, 0:keys]
        dprob = dot_nt(dos, VD[g, 0:keys])
        ds = probs * (dprob - jnp.sum(probs * dprob, axis=-1, keepdims=True))
        low = ds.astype(BF)
        DQ[g, rows] = unstack(dot(low, KD[g, 0:keys])) * HD**-0.5
        dk = dot_tn(low, qs)
        dv = dot_tn(probs.astype(BF), dos)
        if b == 1:
            DK[g] = dk
            DV[g] = dv
        else:
            DK[g, 0:keys] = DK[g, 0:keys] + dk
            DV[g, 0:keys] = DV[g, 0:keys] + dv

    attend_back(0, 1)
    attend_back(0, 0)
    for c in range(2, CHUNKS):
        rs3(c)
    attend_back(1, 1)
    attend_back(1, 0)
    rs4(1)

    def raw_grads(i, carry):
        rows = pl.ds(pl.multiple_of(i * 256, 256), 256)
        dks = DK[:, rows]
        dvs = DV[:, rows]
        dk = jnp.where(left_head, dks[0] + pltpu.roll(dks[0], 64, 1), dks[1] + pltpu.roll(dks[1], 64, 1))
        dv = jnp.where(left_head, dvs[0] + pltpu.roll(dvs[0], 64, 1), dvs[1] + pltpu.roll(dvs[1], 64, 1))
        DQKV[rows, 384:512] = dv.astype(BF)
        sums = []
        for g in range(3):
            e = rope_back(DQ[g, rows] if g < 2 else dk, rows)
            n = NQ[g, rows]
            sums.append(jnp.sum(e * n, axis=0, keepdims=True))
            eg = e * (q_gain if g < 2 else k_gain)
            DQKV[rows, 128 * g : 128 * g + 128] = (
                RQ[g, rows] * (eg - n * head_mean(eg * n))
            ).astype(BF)
        return carry[0] + sums[0] + sums[1], carry[1] + sums[2]

    zero = jnp.zeros((1, 128), F32)
    sum_q, sum_k = lax.fori_loop(0, 2, raw_grads, (zero, zero))
    GV[0, pl.ds(t, 1), :, 2048:2176] = sum_q.reshape(1, 1, 128)
    GV[0, pl.ds(t, 1), :, 2176:2304] = sum_k.reshape(1, 1, 128)

    G0 = Gs[0]

    def attn_grads(i, carry):
        rows = pl.ds(pl.multiple_of(i * 256, 256), 256)
        zs = pl.ds(2 * (i % 2), 2)
        G0[i // 2, zs, :, :, 0:512] = dot(A1T[rows], DQKV[...]).astype(BF).reshape(2, 4, 32, 512)
        return carry

    def out_grads():
        G0[:, :, :, :, 512:768] = (
            dot_tn(GX[...].reshape(512, D), O[...]).astype(BF).reshape(2, 4, 4, 32, 256)
        )

    out_grads()
    lax.fori_loop(0, 4, attn_grads, 0)
    rs1(0)

    def da1_part(b):
        rows = pl.ds(pl.multiple_of(b * 128, 128), 128)
        return dot_nt(DQKV[rows], W0[:, :, :, :, 0:512].reshape(D, 512)).astype(BF)

    da1_copies = sum_start(3, da1_part)
    for c in range(2, CHUNKS):
        rs4(c)
    da1_last = sum_mid(3, da1_copies)
    rs2(0)
    for c in range(1, CHUNKS):
        rs5(c)
    out[...] = (X2[...] + sum_end(2, y_copies, y_last)).astype(BF)
    da1 = sum_end(3, da1_copies, da1_last)
    n1, r1 = rms(tok[...].astype(F32))
    GV[0, pl.ds(t, 1), :, 0:1024] = jnp.sum(da1 * n1, axis=0, keepdims=True).reshape(1, 1, D)
    mine = GV.at[0, t]
    g_copies = [send(mine, mine, device) for device in (d_s, d_o, d_d)]
    h = da1 * na[...]
    gtok[...] = DX2[...] + r1 * (h - n1 * jnp.mean(h * n1, axis=-1, keepdims=True))
    rs3(0)

    def gain_stage(stage, copies, count, place, devices):
        for copy in copies:
            copy.wait_recv()
        total = GV[stage, 0]
        for i in range(1, count):
            total = total + GV[stage, i]
        GV[stage + 1, pl.ds(place, 1)] = total.reshape(1, 1, GAINS)
        v = GV.at[stage + 1, place]
        return [send(v, v, device) for device in devices]

    g_copies = gain_stage(0, g_copies, 4, x, (d_x,))
    rs4(0)
    g_copies = gain_stage(1, g_copies, 2, z, (d_zl, d_zr, d_zo))
    for c in range(1, CHUNKS):
        rs6(c)
    rs5(0)
    g_copies = gain_stage(2, g_copies, 4, y, (d_yl, d_yr, d_yo))
    rs6(0)
    for copy in g_copies:
        copy.wait_recv()
    total = GV[3, 0]
    for i in range(1, 4):
        total = total + GV[3, i]
    turned = pltpu.roll(total[:, 2048:2304], 192, 1) + total[:, 2048:2304]
    gains[:, 0:2048] = total[:, 0:2048]
    gains[:, 2048:2304] = turned

    for copy in started:
        copy.wait_send()


def on_device(
    tokens, seq_lens, norm_attn, w_query, w_key, w_value, w_out, query_gain, key_gain,
    norm_ffn, w_gate, w_up, w_down, cotangent,
):
    freq = np.exp(-math.log(THETA) * 2.0 * np.arange(HD // 2, dtype=np.float64) / HD)
    freq = jnp.asarray(np.tile(freq.astype(np.float32), 4)[None, :])
    shape = jax.ShapeDtypeStruct
    vmem = pl.BlockSpec(memory_space=pltpu.VMEM)
    outs = (
        shape((128, D), BF),
        shape((128, D), F32),
        shape((32, 256), F32),
        shape((32, 128), F32),
        shape((32, 128), F32),
        shape((32, 256), F32),
        shape((32, FFL), F32),
        shape((32, FFL), F32),
        shape((32, FFL), F32),
        shape((1, GAINS), F32),
    )
    V = pltpu.VMEM
    scratch = [
        [V((2, 4, 4, 32, w), BF) for w in WIDTHS],
        [V((2, 4, 4, 32, w), BF) for w in WIDTHS],
        [V((2, 2, 4, 16, w), BF) for w in WIDTHS],
        [V((2, 2, 2, 4, 16, w), BF) for w in WIDTHS],
        [V((2, 2, 16, w), BF) for w in WIDTHS],
        [V((2, 2, 2, 16, w), BF) for w in WIDTHS],
        [V((32, w), BF) for w in WIDTHS],
        V((4, 128, D), BF),
        V((4, 128, D), BF),
        V((4, 128, D), BF),
        V((4, 128, D), BF),
        V((D, 512), BF),
        V((D, 512), BF),
        V((D, 512), BF),
        V((4, 4, 128, D), BF),
        V((4, 2, 128, D), BF),
        V((4, 128, D), BF),
        V((128, D), F32),
        V((128, D), F32),
        V((512, 128), F32),
        V((512, 128), F32),
        V((512, 512), F32),
        V((3, 512, 128), F32),
        V((3, 512, 128), F32),
        V((2, 512, 128), BF),
        V((2, 512, 128), BF),
        V((2, 512, 128), BF),
        V((2, 1024, 512), F32),
        V((512, 256), BF),
        V((512, 256), BF),
        V((2, 512, 128), F32),
        V((2, 512, 128), F32),
        V((2, 512, 128), F32),
        V((512, 512), BF),
        V((512, FFL), BF),
        V((512, FFL), BF),
        V((512, FFL), BF),
        V((512, D), F32),
        V((4, 4, 1, GAINS), F32),
        pltpu.SemaphoreType.DMA((NSEM,)),
        pltpu.SemaphoreType.DMA((NSEM,)),
    ]
    r = pl.pallas_call(
        kernel,
        out_shape=outs,
        in_specs=[pl.BlockSpec(memory_space=pltpu.SMEM)] + [vmem] * 14,
        out_specs=[vmem] * len(outs),
        scratch_shapes=scratch,
        compiler_params=pltpu.CompilerParams(
            collective_id=0, has_side_effects=True, vmem_limit_bytes=63 * 2**20
        ),
        name="layer",
    )(
        seq_lens, tokens, cotangent, w_query, w_key, w_value, w_out.T, w_gate, w_up, w_down.T,
        norm_attn[None], norm_ffn[None], query_gain[None], key_gain[None], freq,
    )
    out, gtok, gq, gk, gv, go, gg, gu, gd, gains = r
    gains = gains[0]
    return (
        out, gtok, gains[0:1024], gq, gk, gv, go.T, gains[2048:2112], gains[2176:2240],
        gains[1024:2048], gg, gu, gd.T,
    )


def solution(mesh):
    rows = P(("dp", "tensor"), None)
    split, across, full = P("dp", "tensor"), P("tensor", "dp"), P()
    return jax.shard_map(
        on_device,
        mesh=mesh,
        in_specs=(
            rows, P("dp", None), full, split, split, split, across, full, full, full,
            split, split, across, rows,
        ),
        out_specs=(
            rows, rows, full, split, split, split, across, full, full, full, split, split, across,
        ),
        check_vma=False,
    )
```

time: 2170 us -> 151 us (0.07)
  waiting for transfers between devices: 1700 us -> 0 us
  blocking collectives: 332 us -> 0 us
  Pallas kernels: 0 us -> 139 us
  matrix products: 78 us -> 0 us
  other arithmetic: 31 us -> 0 us
    reduce_scatter x11 -> x0, waiting for transfers between devices: 1240 us -> none  [the longest x1 163 us: on_device(): lax.psum_scatter(grad_up_w.astype(jnp.bfloat16), 'dp', scatter_dimension=...]
    all_gather x7 -> x0, waiting for transfers between devices: 462 us -> none  [the longest x1 134 us: on_device(): lax.all_gather(w_down, 'dp', axis=1, tiled=True)]
    all_gather x4 -> x0, blocking collectives: 266 us -> none  [the longest x1 71.5 us: on_device(): lax.all_gather(w_key, 'dp', axis=0, tiled=True)]
    pallas_call x0 -> x1, Pallas kernels: none -> 139 us  [on_device(): pl.pallas_call(kernel, out_shape=outs, in_specs=[pl.BlockSpec(memory_spac...]
    dot_general x27 -> x0, matrix products: 78 us -> none  [the longest x7 20 us: mult(): return jnp.dot(left, right, preferred_element_type=jnp.float32)]
    psum x1 -> x0, blocking collectives: 66.2 us -> none  [on_device(): lax.psum((gain_one, gain_query, gain_key, gain_two), ('dp', 'tensor'))]
  transfers between devices with their start and end apart: 18 -> 0, of which waited for: 16 -> 0; matrix products, arithmetic and copies ran while one was open for 4% -> 0% of each run, Pallas kernels for 0% -> 0%
where the time goes in v1:
time: 151 us; the launch traced here: 150 us
  Pallas kernels  139 us (92%)
  local copies, waits for them, and re-layouts  10 us (7%)
    pallas_call x1, Pallas kernels, on_device(): pl.pallas_call(kernel, out_shape=outs, in_specs=[pl.BlockSpec(memory_spac...  139 us
    unnamed x25, local copies, waits for them, and re-layouts  7.52 us

profile of v1, /device:TPU:1, one launch (start us, length us, event | category | flops | bytes accessed | tf_op | source)
XLA Modules:
  0.0 149.5 jit_solution(13332592528012378362)
XLA Ops:
  0.7 138.8 %layer.1 = (bf16[128,1024]{1,0:T(8,128)(2,1)}, f32[128,1024]{1,0:T(8,128)}, f32[32,256]{1,0:T(8,128)}, f32[32,128]{1,0:T(8,128)}, f32[32,128]{1,0:T(8,128)}, /*i...) custom-call(s32[1,4]{1,0:T(1,128)} %lens.1, ...), custom_call_target="tpu_custom_call" | custom-call | tf_op jit(solution)/shard_map/layer/pallas_call | solution.py:735
  139.4 0.0 copy-start
  139.4 1.2 slice_bitcast_fusion
  140.7 1.3 fusion
  142.0 1.7 %copy.37 = bf16[128,1024]{1,0:T(8,128)(2,1)} copy(bf16[128,1024]{1,0:T(8,128)(2,1)} %get-tuple-element.50) | data formatting | bytes 524288
  143.6 0.0 copy-done
  143.6 0.0 copy-start.5
  143.6 0.0 copy-start.7
  143.6 0.0 copy-start.4
  143.7 0.8 copy.38
  144.5 0.0 copy-done.5
  144.5 0.6 copy.39
  145.1 0.0 copy-done.7
  145.1 0.6 copy.40
  145.7 0.0 copy-done.6
  145.7 0.6 copy.41
  146.3 0.0 copy-done.4
  146.3 0.6 copy.42
  146.9 0.0 copy-done.3
  146.9 0.7 copy.43
  147.6 0.3 copy-done.2
  147.9 0.7 copy.44
  148.5 0.3 copy-done.1
  148.8 0.7 copy.45
  (4 shorter events, 0.0 us)
Async XLA Ops:
  139.4 4.2 %copy-start = (f32[128,1024]{1,0:T(8,128)S(1)}, f32[128,1024]{1,0:T(8,128)}, u32[]{:S(2)}) copy-start(f32[128,1024]{1,0:T(8,128)} %get-tuple-element.51) | copy-start | bytes 1572868
  143.6 0.8 copy-start.5
  143.6 1.4 copy-start.7
  143.6 2.0 %copy-start.6 = (f32[32,128]{1,0:T(8,128)S(1)}, f32[32,128]{1,0:T(8,128)}, u32[]{:S(2)}) copy-start(f32[32,128]{1,0:T(8,128)} %get-tuple-element.55) | copy-start | bytes 49156
  143.6 2.6 %copy-start.4 = (f32[32,256]{1,0:T(8,128)S(1)}, f32[32,256]{1,0:T(8,128)}, u32[]{:S(2)}) copy-start(f32[32,256]{1,0:T(8,128)} %get-tuple-element.29) | copy-start | bytes 98308
  144.5 2.5 %copy-start.3 = (f32[32,1152]{1,0:T(8,128)S(1)}, f32[32,1152]{1,0:T(8,128)}, u32[]{:S(2)}) copy-start(f32[32,1152]{1,0:T(8,128)} %get-tuple-element.60) | copy-start | bytes 442372
  146.9 1.0 copy-start.2
  147.9 1.0 copy-start.1

commit v2 on v1

--- a/solution.py
+++ b/solution.py
@@ -15,15 +15,17 @@
 
 D = 1024
 HD = 64
-FF_PARTS = (384, 384, 384)
+FF_PARTS = (256, 512, 384)
 FF_OFF = tuple(int(v) for v in np.cumsum((0,) + FF_PARTS)[:-1])
 WIDTHS = (768,) + tuple(3 * c for c in FF_PARTS)
 CHUNKS = len(WIDTHS)
+OUT = CHUNKS
+SUMS = (512,) + WIDTHS[1:] + (256,)
 FFL = sum(FF_PARTS)
 EPS = 1e-05
 THETA = 1000000.0
 GAINS = 2304
-NSEM = 34 * CHUNKS + 40
+NSEM = 17 * CHUNKS + 17 * len(SUMS) + 50
 
 LO = pl.ds(0, 16)
 HI = pl.ds(16, 16)
@@ -48,12 +50,12 @@
 
 def kernel(
     lens, tok, cot, wq, wk, wv, wo, wg, wu, wd, na, nf, qg, kg, fr,
-    out, gtok, gq_w, gk_w, gv_w, go_w, gg_w, gu_w, gd_w, gains,
+    out, gtok, gq_w, gk_w, gv_w, go_w, gg_w, gu_w, gd_w, gna, gnf, gqg, gkg,
     Ws, Gs, RA, RB, RC, RD, RE,
     A1, A2, GO, GX, A1T, A2T, GOT,
     PB, T1, T2, X2, DX2,
     COS, SIN, BIAS, NQ, RQ, QS, KD, VD, PR, O, DO, DQ, DK, DV, DQKV,
-    HID, DG, DU, DA, GV,
+    HID, DG, DU, DA, GVA, GVB,
     ssem, rsem,
 ):
     me = lax.axis_index("dp")
@@ -75,8 +77,14 @@
     d_zl, d_zr, d_zo = dp(x, zl, y), dp(x, zr, y), dp(x, zo, y)
     d_yl, d_yr, d_yo = dp(x, z, yl), dp(x, z, yr), dp(x, z, yo)
     d_s, d_o, d_d = (me, ts), (me, to), (me, td)
-    partners = (d_x, d_zl, d_zr, d_zo, d_yl, d_yr, d_yo, d_s, d_o, d_d)
-
+    ring_z, ring_y = (d_zr, d_zl, d_zo), (d_yr, d_yl, d_yo)
+    near = (d_s, d_o, d_d, d_x) + tuple((d_x[0], other) for other in (ts, to, td))
+    plane = tuple(
+        dp(x, (z + i) % 4, (y + j) % 4) for i in range(4) for j in range(4) if i or j
+    )
+    partners = near + plane
+
+    slot = x * 4 + t
     started = []
 
     def send(src, dst, device):
@@ -152,7 +160,22 @@
         for copy in ag[c, 4]:
             copy.wait_recv()
 
-    ag_steps = (ag0, ag1, ag2, ag3, ag4, ag5)
+    def ag1_direct(c):
+        W = Ws[c]
+        ag[c, 0].wait_recv()
+        a, b = W.at[:, z, y, LO], W.at[:, z, y, HI]
+        ag[c, 1] = [send(a, a, d) for d in ring_z], [send(b, b, d) for d in ring_y]
+
+    def ag2_direct(c):
+        W = Ws[c]
+        for copy in ag[c, 1][0]:
+            copy.wait_recv()
+        a = W.at[:, :, y, LO]
+        first = [send(a, a, d) for d in ring_y]
+        for copy in ag[c, 1][1]:
+            copy.wait_recv()
+        b = W.at[:, z, :, HI]
+        ag[c, 4] = first + [send(b, b, d) for d in ring_z]
 
     rs = {}
 
@@ -238,14 +261,39 @@
             gq_w[...] = total[:, 0:256]
             gk_w[...] = total[:, 256:384]
             gv_w[...] = total[:, 384:512]
-            go_w[...] = total[:, 512:768]
+        elif c == OUT:
+            go_w[...] = total
         else:
             w, o = FF_PARTS[c - 1], FF_OFF[c - 1]
             gg_w[:, o : o + w] = total[:, 0:w]
             gu_w[:, o : o + w] = total[:, w : 2 * w]
             gd_w[:, o : o + w] = total[:, 2 * w : 3 * w]
 
-    rs_steps = (None, rs1, rs2, rs3, rs4, rs5, rs6)
+    def rs1_direct(c):
+        G, rb = Gs[c], RB[c]
+        a = [send(G.at[:, :, i, LO], rb.at[0, k], d) for k, (i, d) in enumerate(zip((yr, yl, yo), ring_y))]
+        b = [send(G.at[:, i, :, HI], rb.at[1, k], d) for k, (i, d) in enumerate(zip((zr, zl, zo), ring_z))]
+        rs[c, 2] = a, b
+
+    def rs3_direct(c):
+        G, rb, rd, (a, b) = Gs[c], RB[c], RD[c], rs[c, 2]
+        for copy in a:
+            copy.wait_recv()
+        add(G, (every, every, one(y), lo), rb[0, 0], rb[0, 1], rb[0, 2])
+        a = [send(G.at[:, i, y, LO], rd.at[0, k], d) for k, (i, d) in enumerate(zip((zr, zl, zo), ring_z))]
+        for copy in b:
+            copy.wait_recv()
+        add(G, (every, one(z), every, hi), rb[1, 0], rb[1, 1], rb[1, 2])
+        b = [send(G.at[:, z, i, HI], rd.at[1, k], d) for k, (i, d) in enumerate(zip((yr, yl, yo), ring_y))]
+        rs[c, 4] = a + b
+
+    def rs5_direct(c):
+        G, rd = Gs[c], RD[c]
+        for copy in rs[c, 4]:
+            copy.wait_recv()
+        add(G, (every, one(z), one(y), lo), rd[0, 0], rd[0, 1], rd[0, 2])
+        add(G, (every, one(z), one(y), hi), rd[1, 0], rd[1, 1], rd[1, 2])
+        rs[c, 5] = send(G.at[xo, z, y], RE[c], d_x)
 
     def rows_start(buf):
         v = buf.at[t]
@@ -260,14 +308,20 @@
         pair[1].wait_recv()
         relay.wait_recv()
 
+    def sum_far(k, part):
+        PB[k, td] = part(td)
+        copy = send(PB.at[k, td], T1.at[k, 1], d_s)
+        PB[k, to] = part(to)
+        return (copy,)
+
+    def sum_near(k, part):
+        PB[k, ts] = part(ts)
+        copy = send(PB.at[k, ts], T1.at[k, 0], d_s)
+        PB[k, t] = part(t)
+        return (copy,)
+
     def sum_start(k, part):
-        PB[k, td] = part(td)
-        c0 = send(PB.at[k, td], T1.at[k, 1], d_s)
-        PB[k, ts] = part(ts)
-        c1 = send(PB.at[k, ts], T1.at[k, 0], d_s)
-        PB[k, to] = part(to)
-        PB[k, t] = part(t)
-        return c0, c1
+        return sum_far(k, part) + sum_near(k, part)
 
     def sum_mid(k, copies):
         copies[0].wait_recv()
@@ -334,25 +388,24 @@
         BIAS[rows] = jnp.where(seen, 0.0, -1e30)
         return carry
 
-    ag1(0)
     lax.fori_loop(0, 4, fill_tables, 0)
+    ag1_direct(0)
     a1_relay = rows_relay(A1, a1_pair)
-    ag2(0)
-    go_pair = rows_start(GO)
     ag1(1)
     lax.fori_loop(0, 4, fill_bias, 0)
-    ag3(0)
+    ag2_direct(0)
     rows_end(a1_pair, a1_relay)
     ag2(1)
-    A1T[...] = A1[...].reshape(512, D).T
-    go_relay = rows_relay(GO, go_pair)
     for c in range(2, CHUNKS):
         ag1(c)
-    ag4(0)
+    A1T[...] = A1[...].reshape(512, D).T
     ag3(1)
-    rows_end(go_pair, go_relay)
-    GOT[...] = GO[...].reshape(512, D).T
+    for c in range(2, CHUNKS):
+        ag2(c)
     ag5(0)
+    go_pair = rows_start(GO)
+    for c in range(2, CHUNKS):
+        ag3(c)
 
     def rope(v, rows):
         swapped = jnp.where(first_half, pltpu.roll(v, 96, 1), pltpu.roll(v, 32, 1))
@@ -408,35 +461,35 @@
         half = v.shape[0] // 2
         return jnp.where(left_head, v[:half], v[half:])
 
-    def attend(g, b):
-        rows, keys = pl.ds(256 * b, 256), 256 * (b + 1)
-        scores = dot_nt(stack(QS[g, rows]), KD[g, 0:keys])
-        bias = BIAS[rows, 0:keys]
+    def attend(g, i):
+        rows = pl.ds(pl.multiple_of(i * 256, 256), 256)
+        scores = dot_nt(stack(QS[g, rows]), KD[g])
+        bias = BIAS[rows]
         scores = scores + jnp.concatenate([bias, bias], axis=0)
         expo = jnp.exp(scores - jnp.max(scores, axis=-1, keepdims=True))
         probs = expo * (1.0 / jnp.sum(expo, axis=-1, keepdims=True))
-        PR[g, 512 * b : 512 * b + 512, 0:keys] = probs
-        O[rows, 128 * g : 128 * g + 128] = unstack(dot(probs.astype(BF), VD[g, 0:keys])).astype(BF)
-
-    ag4(1)
-    attend(0, 0)
-    attend(0, 1)
-    ag2(2)
-    attend(1, 0)
-    attend(1, 1)
-    ag3(2)
+        PR[g, pl.ds(pl.multiple_of(i * 512, 512), 512)] = probs
+        O[rows, 128 * g : 128 * g + 128] = unstack(dot(probs.astype(BF), VD[g])).astype(BF)
+
+    here = t // 2
+    there = 1 - here
 
     def out_part(b):
         rows = pl.ds(pl.multiple_of(b * 128, 128), 128)
         return dot_nt(O[rows], W0[:, :, :, :, 512:768].reshape(D, 256)).astype(BF)
 
-    at_copies = sum_start(0, out_part)
-    for c in range(3, CHUNKS):
-        ag2(c)
+    attend(0, there)
+    attend(1, there)
+    at_copies = sum_far(0, out_part)
+    ag4(1)
+    go_relay = rows_relay(GO, go_pair)
+    attend(0, here)
     at_last = sum_mid(0, at_copies)
+    attend(1, here)
+    at_copies += sum_near(0, out_part)
+    rows_end(go_pair, go_relay)
+    GOT[...] = GO[...].reshape(512, D).T
     ag4(2)
-    for c in range(3, CHUNKS):
-        ag3(c)
     x2 = tok[...].astype(F32) + sum_end(0, at_copies, at_last)
     X2[...] = x2
     n2, _ = rms(x2)
@@ -445,39 +498,32 @@
     ag5(1)
     for c in range(3, CHUNKS):
         ag4(c)
-    a2_relay = rows_relay(A2, a2_pair)
-    rows_end(a2_pair, a2_relay)
-    A2T[...] = A2[...].reshape(512, D).T
-
-    def ffn_chunk(c):
-        W, G = Ws[c], Gs[c]
+
+    def ffn_chunk(c, i):
+        W = Ws[c]
         w, o = FF_PARTS[c - 1], FF_OFF[c - 1]
         cols = slice(o, o + w)
 
-        def block(i, carry):
-            rows = pl.ds(pl.multiple_of(i * 256, 256), 256)
-            a = A2[pl.ds(2 * i, 2)].reshape(256, D)
-            g = GO[pl.ds(2 * i, 2)].reshape(256, D)
-            gate = dot(a, W[:, :, :, :, 0:w].reshape(D, w))
-            up = dot(a, W[:, :, :, :, w : 2 * w].reshape(D, w))
-            dhid = dot(g, W[:, :, :, :, 2 * w : 3 * w].reshape(D, w))
-            sigma = jax.nn.sigmoid(gate)
-            swish = gate * sigma
-            HID[rows, cols] = (swish * up).astype(BF)
-            dgate = (dhid * up * sigma * (1.0 + gate * (1.0 - sigma))).astype(BF)
-            dup = (dhid * swish).astype(BF)
-            DG[rows, cols] = dgate
-            DU[rows, cols] = dup
-            part = dot_nt(dgate, W[:, :, :, :, 0:w].reshape(D, w)) + dot_nt(
-                dup, W[:, :, :, :, w : 2 * w].reshape(D, w)
-            )
-            if c == 1:
-                DA[rows] = part
-            else:
-                DA[rows] = DA[rows] + part
-            return carry
-
-        lax.fori_loop(0, 2, block, 0)
+        rows = pl.ds(pl.multiple_of(i * 256, 256), 256)
+        a = A2[pl.ds(2 * i, 2)].reshape(256, D)
+        g = GO[pl.ds(2 * i, 2)].reshape(256, D)
+        gate = dot(a, W[:, :, :, :, 0:w].reshape(D, w))
+        up = dot(a, W[:, :, :, :, w : 2 * w].reshape(D, w))
+        dhid = dot(g, W[:, :, :, :, 2 * w : 3 * w].reshape(D, w))
+        sigma = jax.nn.sigmoid(gate)
+        swish = gate * sigma
+        HID[rows, cols] = (swish * up).astype(BF)
+        dgate = (dhid * up * sigma * (1.0 + gate * (1.0 - sigma))).astype(BF)
+        dup = (dhid * swish).astype(BF)
+        DG[rows, cols] = dgate
+        DU[rows, cols] = dup
+        part = dot_nt(dgate, W[:, :, :, :, 0:w].reshape(D, w)) + dot_nt(
+            dup, W[:, :, :, :, w : 2 * w].reshape(D, w)
+        )
+        if c == 1:
+            DA[rows] = part
+        else:
+            DA[rows] = DA[rows] + part
 
     def ffn_grads(c):
         G = Gs[c]
@@ -495,26 +541,34 @@
 
         lax.fori_loop(0, 4, block, 0)
 
-    for c in range(1, CHUNKS):
-        if c > 1:
-            ag5(c)
-        ffn_chunk(c)
-        if c + 1 < CHUNKS:
-            ffn_grads(c)
-            rs1(c)
-            if c > 1:
-                rs2(c - 1)
-
     def da2_part(b):
         rows = pl.ds(pl.multiple_of(b * 128, 128), 128)
         return DA[rows].astype(BF)
 
-    da2_copies = sum_start(1, da2_part)
-    ffn_grads(CHUNKS - 1)
-    rs1(CHUNKS - 1)
+    a2_pair[1].wait_recv()
+    ffn_chunk(1, here)
+    a2_relay = rows_relay(A2, a2_pair)
+    ag5(2)
+    ffn_chunk(2, here)
+    a2_relay.wait_recv()
+    A2T[...] = A2[...].reshape(512, D).T
+    ffn_chunk(1, there)
+    ffn_grads(1)
+    rs1(1)
+    for c in range(2, CHUNKS):
+        if c > 2:
+            ag5(c)
+        ffn_chunk(c, there)
+        if c + 1 == CHUNKS:
+            da2_copies = sum_far(1, da2_part)
+        if c > 2:
+            ffn_chunk(c, here)
+    da2_copies += sum_near(1, da2_part)
     da2_last = sum_mid(1, da2_copies)
-    if CHUNKS > 2:
-        rs2(CHUNKS - 2)
+    rs2(1)
+    for c in range(2, CHUNKS):
+        ffn_grads(c)
+        rs1(c)
 
     def y_part(b):
         rows = pl.ds(pl.multiple_of(b * 128, 128), 128)
@@ -525,56 +579,56 @@
             total = part if total is None else total + part
         return total.astype(BF)
 
-    y_copies = sum_start(2, y_part)
-
     da2 = sum_end(1, da2_copies, da2_last)
     n2, r2 = rms(X2[...])
-    GV[0, pl.ds(t, 1), :, 1024:2048] = jnp.sum(da2 * n2, axis=0, keepdims=True).reshape(1, 1, D)
+    GVA[pl.ds(slot, 1), :, 1024:2048] = jnp.sum(da2 * n2, axis=0, keepdims=True).reshape(1, 1, D)
     h = da2 * nf[...]
     dx2 = cot[...].astype(F32) + r2 * (h - n2 * jnp.mean(h * n2, axis=-1, keepdims=True))
     DX2[...] = dx2
     GX[t] = dx2.astype(BF)
     gx_pair = rows_start(GX)
-    rs2(CHUNKS - 1)
-    gx_relay = rows_relay(GX, gx_pair)
-    y_last = sum_mid(2, y_copies)
-    if CHUNKS > 2:
-        rs3(1)
-    rows_end(gx_pair, gx_relay)
-
-    def do_block(i, carry):
+    rs2(2)
+    y_copies = sum_far(2, y_part)
+
+    def do_block(i):
         rows = pl.ds(pl.multiple_of(i * 256, 256), 256)
         g = GX[pl.ds(2 * i, 2)].reshape(256, D)
         DO[rows] = dot(g, W0[:, :, :, :, 512:768].reshape(D, 256)).astype(BF)
-        return carry
-
-    lax.fori_loop(0, 2, do_block, 0)
-
-    def attend_back(g, b):
-        rows, keys = pl.ds(256 * b, 256), 256 * (b + 1)
+
+    def attend_back(g, i, first):
+        rows = pl.ds(pl.multiple_of(i * 256, 256), 256)
         qs = stack(QS[g, rows])
         dos = stack(DO[rows, 128 * g : 128 * g + 128])
-        probs = PR[g, 512 * b : 512 * b + 512, 0:keys]
-        dprob = dot_nt(dos, VD[g, 0:keys])
+        probs = PR[g, pl.ds(pl.multiple_of(i * 512, 512), 512)]
+        dprob = dot_nt(dos, VD[g])
         ds = probs * (dprob - jnp.sum(probs * dprob, axis=-1, keepdims=True))
         low = ds.astype(BF)
-        DQ[g, rows] = unstack(dot(low, KD[g, 0:keys])) * HD**-0.5
+        DQ[g, rows] = unstack(dot(low, KD[g])) * HD**-0.5
         dk = dot_tn(low, qs)
         dv = dot_tn(probs.astype(BF), dos)
-        if b == 1:
+        if first:
             DK[g] = dk
             DV[g] = dv
         else:
-            DK[g, 0:keys] = DK[g, 0:keys] + dk
-            DV[g, 0:keys] = DV[g, 0:keys] + dv
-
-    attend_back(0, 1)
-    attend_back(0, 0)
-    for c in range(2, CHUNKS):
-        rs3(c)
-    attend_back(1, 1)
-    attend_back(1, 0)
-    rs4(1)
+            DK[g] = DK[g] + dk
+            DV[g] = DV[g] + dv
+
+    gx_pair[1].wait_recv()
+    do_block(here)
+    attend_back(0, here, True)
+    gx_relay = rows_relay(GX, gx_pair)
+    attend_back(1, here, True)
+    y_copies += sum_near(2, y_part)
+    for c in range(3, CHUNKS):
+        rs2(c)
+    gx_relay.wait_recv()
+    do_block(there)
+    Gs[OUT][...] = dot_tn(GX[...].reshape(512, D), O[...]).astype(BF).reshape(2, 4, 4, 32, 256)
+    rs1_direct(OUT)
+    attend_back(0, there, False)
+    rs3(1)
+    attend_back(1, there, False)
+    rs3(2)
 
     def raw_grads(i, carry):
         rows = pl.ds(pl.multiple_of(i * 256, 256), 256)
@@ -596,8 +650,8 @@
 
     zero = jnp.zeros((1, 128), F32)
     sum_q, sum_k = lax.fori_loop(0, 2, raw_grads, (zero, zero))
-    GV[0, pl.ds(t, 1), :, 2048:2176] = sum_q.reshape(1, 1, 128)
-    GV[0, pl.ds(t, 1), :, 2176:2304] = sum_k.reshape(1, 1, 128)
+    GVA[pl.ds(slot, 1), :, 2048:2176] = sum_q.reshape(1, 1, 128)
+    GVA[pl.ds(slot, 1), :, 2176:2304] = sum_k.reshape(1, 1, 128)
 
     G0 = Gs[0]
 
@@ -607,65 +661,74 @@
         G0[i // 2, zs, :, :, 0:512] = dot(A1T[rows], DQKV[...]).astype(BF).reshape(2, 4, 32, 512)
         return carry
 
-    def out_grads():
-        G0[:, :, :, :, 512:768] = (
-            dot_tn(GX[...].reshape(512, D), O[...]).astype(BF).reshape(2, 4, 4, 32, 256)
-        )
-
-    out_grads()
-    lax.fori_loop(0, 4, attn_grads, 0)
-    rs1(0)
-
     def da1_part(b):
         rows = pl.ds(pl.multiple_of(b * 128, 128), 128)
         return dot_nt(DQKV[rows], W0[:, :, :, :, 0:512].reshape(D, 512)).astype(BF)
 
     da1_copies = sum_start(3, da1_part)
-    for c in range(2, CHUNKS):
+    lax.fori_loop(0, 4, attn_grads, 0)
+    rs1_direct(0)
+    da1_last = sum_mid(3, da1_copies)
+    rs3_direct(OUT)
+    rs4(1)
+    for c in range(3, CHUNKS):
+        rs3(c)
+    y_last = sum_mid(2, y_copies)
+    rs4(2)
+    rs5(1)
+    rs3_direct(0)
+    rs5_direct(OUT)
+    for c in range(3, CHUNKS):
         rs4(c)
-    da1_last = sum_mid(3, da1_copies)
-    rs2(0)
-    for c in range(1, CHUNKS):
+    rs5(2)
+    da1 = sum_end(3, da1_copies, da1_last)
+    n1, r1 = rms(tok[...].astype(F32))
+    GVA[pl.ds(slot, 1), :, 0:1024] = jnp.sum(da1 * n1, axis=0, keepdims=True).reshape(1, 1, D)
+    mine = GVA.at[slot]
+    g_copies = [send(mine, mine, device) for device in near]
+    h = da1 * na[...]
+    gtok[...] = DX2[...] + r1 * (h - n1 * jnp.mean(h * n1, axis=-1, keepdims=True))
+    rs5_direct(0)
+
+    def total_of(ref, count, copies):
+        for copy in copies:
+            copy.wait_recv()
+        total = ref[0]
+        for i in range(1, count):
+            total = total + ref[i]
+        return total
+
+    GVB[pl.ds(z * 4 + y, 1)] = total_of(GVA, 8, g_copies).reshape(1, 1, GAINS)
+    mine = GVB.at[z * 4 + y]
+    g_copies = [send(mine, mine, device) for device in plane]
+    for c in range(3, CHUNKS):
         rs5(c)
     out[...] = (X2[...] + sum_end(2, y_copies, y_last)).astype(BF)
-    da1 = sum_end(3, da1_copies, da1_last)
-    n1, r1 = rms(tok[...].astype(F32))
-    GV[0, pl.ds(t, 1), :, 0:1024] = jnp.sum(da1 * n1, axis=0, keepdims=True).reshape(1, 1, D)
-    mine = GV.at[0, t]
-    g_copies = [send(mine, mine, device) for device in (d_s, d_o, d_d)]
-    h = da1 * na[...]
-    gtok[...] = DX2[...] + r1 * (h - n1 * jnp.mean(h * n1, axis=-1, keepdims=True))
-    rs3(0)
-
-    def gain_stage(stage, copies, count, place, devices):
-        for copy in copies:
-            copy.wait_recv()
-        total = GV[stage, 0]
-        for i in range(1, count):
-            total = total + GV[stage, i]
-        GV[stage + 1, pl.ds(place, 1)] = total.reshape(1, 1, GAINS)
-        v = GV.at[stage + 1, place]
-        return [send(v, v, device) for device in devices]
-
-    g_copies = gain_stage(0, g_copies, 4, x, (d_x,))
-    rs4(0)
-    g_copies = gain_stage(1, g_copies, 2, z, (d_zl, d_zr, d_zo))
     for c in range(1, CHUNKS):
         rs6(c)
-    rs5(0)
-    g_copies = gain_stage(2, g_copies, 4, y, (d_yl, d_yr, d_yo))
+    rs6(OUT)
     rs6(0)
-    for copy in g_copies:
-        copy.wait_recv()
-    total = GV[3, 0]
-    for i in range(1, 4):
-        total = total + GV[3, i]
+    total = total_of(GVB, 16, g_copies)
     turned = pltpu.roll(total[:, 2048:2304], 192, 1) + total[:, 2048:2304]
-    gains[:, 0:2048] = total[:, 0:2048]
-    gains[:, 2048:2304] = turned
+    gna[...] = total[:, 0:1024]
+    gnf[...] = total[:, 1024:2048]
+    gqg[...] = turned[:, 0:64]
+    gkg[...] = turned[:, 128:192]
 
     for copy in started:
         copy.wait_send()
+
+
+def hand_on(*refs):
+    count = len(refs) // 2
+    sems = refs[-1]
+    copies = [
+        pltpu.make_async_copy(refs[i], refs[count + i], sems.at[i]) for i in range(count)
+    ]
+    for copy in copies:
+        copy.start()
+    for copy in copies:
+        copy.wait()
 
 
 def on_device(
@@ -686,17 +749,20 @@
         shape((32, FFL), F32),
         shape((32, FFL), F32),
         shape((32, FFL), F32),
-        shape((1, GAINS), F32),
+        shape((1, D), F32),
+        shape((1, D), F32),
+        shape((1, HD), F32),
+        shape((1, HD), F32),
     )
     V = pltpu.VMEM
     scratch = [
         [V((2, 4, 4, 32, w), BF) for w in WIDTHS],
-        [V((2, 4, 4, 32, w), BF) for w in WIDTHS],
-        [V((2, 2, 4, 16, w), BF) for w in WIDTHS],
-        [V((2, 2, 2, 4, 16, w), BF) for w in WIDTHS],
-        [V((2, 2, 16, w), BF) for w in WIDTHS],
-        [V((2, 2, 2, 16, w), BF) for w in WIDTHS],
-        [V((32, w), BF) for w in WIDTHS],
+        [V((2, 4, 4, 32, w), BF) for w in SUMS],
+        [V((2, 2, 4, 16, w) if 0 < i < OUT else (16, 128), BF) for i, w in enumerate(SUMS)],
+        [V((2, 2 if 0 < i < OUT else 3, 2, 4, 16, w), BF) for i, w in enumerate(SUMS)],
+        [V((2, 2, 16, w) if 0 < i < OUT else (16, 128), BF) for i, w in enumerate(SUMS)],
+        [V((2, 2 if 0 < i < OUT else 3, 2, 16, w), BF) for i, w in enumerate(SUMS)],
+        [V((32, w), BF) for w in SUMS],
         V((4, 128, D), BF),
         V((4, 128, D), BF),
         V((4, 128, D), BF),
@@ -728,7 +794,8 @@
         V((512, FFL), BF),
         V((512, FFL), BF),
         V((512, D), F32),
-        V((4, 4, 1, GAINS), F32),
+        V((8, 1, GAINS), F32),
+        V((16, 1, GAINS), F32),
         pltpu.SemaphoreType.DMA((NSEM,)),
         pltpu.SemaphoreType.DMA((NSEM,)),
     ]
@@ -746,12 +813,17 @@
         seq_lens, tokens, cotangent, w_query, w_key, w_value, w_out.T, w_gate, w_up, w_down.T,
         norm_attn[None], norm_ffn[None], query_gain[None], key_gain[None], freq,
     )
-    out, gtok, gq, gk, gv, go, gg, gu, gd, gains = r
-    gains = gains[0]
-    return (
-        out, gtok, gains[0:1024], gq, gk, gv, go.T, gains[2048:2112], gains[2176:2240],
-        gains[1024:2048], gg, gu, gd.T,
-    )
+    anywhere = pl.BlockSpec(memory_space=pl.ANY)
+    r = pl.pallas_call(
+        hand_on,
+        out_shape=outs,
+        in_specs=[vmem] * len(outs),
+        out_specs=[anywhere] * len(outs),
+        scratch_shapes=[pltpu.SemaphoreType.DMA((len(outs),))],
+        name="hand_on",
+    )(*r)
+    out, gtok, gq, gk, gv, go, gg, gu, gd, gna, gnf, gqg, gkg = r
+    return (out, gtok, gna[0], gq, gk, gv, go.T, gqg[0], gkg[0], gnf[0], gg, gu, gd.T)
 
 
 def solution(mesh):

time: 151 us -> 137 us (0.907)
  local copies, waits for them, and re-layouts: 10 us -> 0 us
  Pallas kernels: 139 us -> 136 us
    unnamed x25 -> x0, local copies, waits for them, and re-layouts: 7.52 us -> none
    pallas_call x1, Pallas kernels: 139 us -> 133 us  [on_device(): pl.pallas_call(kernel, out_shape=outs, in_specs=[pl.BlockSpec(memory_spac...]
    slice x2 -> x0, local copies, waits for them, and re-layouts: 2.53 us -> none  [the longest x1 1.28 us: on_device(): gains[1024:2048]]
    pallas_call x0 -> x1, Pallas kernels: none -> 2.5 us  [on_device(): pl.pallas_call(hand_on, out_shape=outs, in_specs=[vmem] * len(outs), out_...]
where the time goes in v2:
time: 137 us
  Pallas kernels  136 us (99%)
    pallas_call x1, Pallas kernels, on_device(): pl.pallas_call(kernel, out_shape=outs, in_specs=[pl.BlockSpec(memory_spac...  133 us

profile of v2, /device:TPU:1, one launch (start us, length us, event | category | flops | bytes accessed | tf_op | source)
XLA Modules:
  0.0 136.5 jit_solution(16912529044987308847)
XLA Ops:
  0.7 133.2 %layer.1 = (bf16[128,1024]{1,0:T(8,128)(2,1)}, f32[128,1024]{1,0:T(8,128)}, f32[32,256]{1,0:T(8,128)}, f32[32,128]{1,0:T(8,128)}, f32[32,128]{1,0:T(8,128)}, /*i...) custom-call(s32[1,4]{1,0:T(1,128)} %lens.1, ...), custom_call_target="tpu_custom_call" | custom-call | tf_op jit(solution)/shard_map/layer/pallas_call | solution.py:802
  133.9 2.5 %hand_on.1 = (bf16[128,1024]{1,0:T(8,128)(2,1)}, f32[128,1024]{1,0:T(8,128)}, f32[32,256]{1,0:T(8,128)}, f32[32,128]{1,0:T(8,128)}, f32[32,128]{1,0:T(8,128)}, /...) custom-call(bf16[128,1024]{1,0:T(8,128)(2,1)} %get-tuple-element.39., ...), custom_call_target="tpu_custom_call" | custom-call | tf_op jit(solution)/shard_map/hand_on/pallas_call | solution.py:817

commit v3 on v2

--- a/solution.py
+++ b/solution.py
@@ -388,20 +388,19 @@
         BIAS[rows] = jnp.where(seen, 0.0, -1e30)
         return carry
 
-    lax.fori_loop(0, 4, fill_tables, 0)
+    lax.fori_loop(0, 2, fill_tables, 0)
     ag1_direct(0)
+    lax.fori_loop(2, 4, fill_tables, 0)
+    ag2_direct(0)
     a1_relay = rows_relay(A1, a1_pair)
-    ag1(1)
+    for c in range(1, CHUNKS):
+        ag1(c)
     lax.fori_loop(0, 4, fill_bias, 0)
-    ag2_direct(0)
     rows_end(a1_pair, a1_relay)
-    ag2(1)
-    for c in range(2, CHUNKS):
-        ag1(c)
     A1T[...] = A1[...].reshape(512, D).T
+    for c in range(1, CHUNKS):
+        ag2(c)
     ag3(1)
-    for c in range(2, CHUNKS):
-        ag2(c)
     ag5(0)
     go_pair = rows_start(GO)
     for c in range(2, CHUNKS):
@@ -579,6 +578,7 @@
             total = part if total is None else total + part
         return total.astype(BF)
 
+    rs2(2)
     da2 = sum_end(1, da2_copies, da2_last)
     n2, r2 = rms(X2[...])
     GVA[pl.ds(slot, 1), :, 1024:2048] = jnp.sum(da2 * n2, axis=0, keepdims=True).reshape(1, 1, D)
@@ -587,7 +587,6 @@
     DX2[...] = dx2
     GX[t] = dx2.astype(BF)
     gx_pair = rows_start(GX)
-    rs2(2)
     y_copies = sum_far(2, y_part)
 
     def do_block(i):

time: 137 us -> 134 us (0.978)
  Pallas kernels: 136 us -> 133 us
    pallas_call x1, Pallas kernels: 133 us -> 130 us  [on_device(): pl.pallas_call(kernel, out_shape=outs, in_specs=[pl.BlockSpec(memory_spac...]
where the time goes in v3:
time: 134 us
  Pallas kernels  133 us (99%)
    pallas_call x1, Pallas kernels, on_device(): pl.pallas_call(kernel, out_shape=outs, in_specs=[pl.BlockSpec(memory_spac...  130 us

profile of v3, /device:TPU:1, one launch (start us, length us, event | category | flops | bytes accessed | tf_op | source)
XLA Modules:
  0.0 133.6 jit_solution(13064004009756526574)
XLA Ops:
  0.7 130.3 %layer.1 = (bf16[128,1024]{1,0:T(8,128)(2,1)}, f32[128,1024]{1,0:T(8,128)}, f32[32,256]{1,0:T(8,128)}, f32[32,128]{1,0:T(8,128)}, f32[32,128]{1,0:T(8,128)}, /*i...) custom-call(s32[1,4]{1,0:T(1,128)} %lens.1, ...), custom_call_target="tpu_custom_call" | custom-call | tf_op jit(solution)/shard_map/layer/pallas_call | solution.py:801
  130.9 2.5 %hand_on.1 = (bf16[128,1024]{1,0:T(8,128)(2,1)}, f32[128,1024]{1,0:T(8,128)}, f32[32,256]{1,0:T(8,128)}, f32[32,128]{1,0:T(8,128)}, f32[32,128]{1,0:T(8,128)}, /...) custom-call(bf16[128,1024]{1,0:T(8,128)(2,1)} %get-tuple-element.39., ...), custom_call_target="tpu_custom_call" | custom-call | tf_op jit(solution)/shard_map/hand_on/pallas_call | solution.py:816
